TPU v7x, 768 devices: a whole 4x8x12 slice. The times are simulated.
768 devices in a mesh: dp: 192 (over y, z_lo, x), seq: 4 (over z_hi, core).
Axes of the slice: x: 4, y: 8, z: 12 (z_hi: 2, z_lo: 6; z = z_hi * 6 + z_lo), core: 2. Of those that a mesh axis runs over, the one named last changes fastest.
Arguments:
- query_states: bfloat16 [98304, 4096], P(('dp', 'seq')), may hold values from -2.5 to 2.5
- key_states: bfloat16 [98304, 1024], P(('dp', 'seq')), may hold values from -2.5 to 2.5
- value_states: bfloat16 [98304, 1024], P(('dp', 'seq')), may hold values from -4 to 4
- residual: bfloat16 [98304, 4096], P(('dp', 'seq')), may hold values from -41 to 41
- norm_gain: float32 [4096], replicated, may hold values from 0.1 to 1.9
- reward_head: float32 [4096], replicated, may hold values from -0.09375 to 0.09375
- lengths: int32 [192, 8], P('dp'), may hold values from 1 to 128, 512 in all within a row
- response_slot: int32 [1536], replicated, may hold values from 0 to 1535, each once
Outputs:
- mean_loss: float32 [], replicated
- query_grad: bfloat16 [98304, 4096], P(('dp', 'seq'))
- key_grad: bfloat16 [98304, 1024], P(('dp', 'seq'))
- value_grad: bfloat16 [98304, 1024], P(('dp', 'seq'))
- gain_grad: float32 [4096], replicated
- head_grad: float32 [4096], replicated
Inputs may be any that keep to these rules, and one draw needn't show every extreme that they name: Each row lists the lengths of the 8 responses packed in that window, in order; they sum to 512 and the largest is exactly 128. `response_slot`: every value appears once.
All inputs are finite; a program needn't handle non-finite values.
Results may differ from a plain program's by a relative error of at most 0.0069.
Values may be sent and summed in bfloat16 or wider, within the bound.
No kernel may reach another device: no remote copies, remote signals or barrier semaphores. Data moves between devices by JAX's collectives and lax.ppermute only.
A program may use at most 64 MiB of HBM per device.

v0:
```python
import jax
import jax.numpy as jnp
from jax import lax
from jax.sharding import PartitionSpec as P

H = 32
KVH = 8
HD = 128
KVD = 1024
DOCS = 8
GROUP = 16


loss_scale = 8192.0
norm_eps = 1e-05


def passed_along(block, axis, distance):
    devices = range(lax.axis_size(axis))
    route = [(i - distance, i) for i in devices if i - distance in devices]
    return lax.ppermute(block, axis, route)


def document_index(length_row, positions):
    ends = jnp.cumsum(length_row)
    return jnp.sum((positions[:, None] >= ends[None, :]).astype(jnp.int32), axis=1)


def plackett(rewards, response_slot):
    ordered = jnp.zeros(rewards.shape, rewards.dtype).at[response_slot].set(rewards)
    rank_grid = ordered.reshape(-1, GROUP)
    raised = jnp.exp(rank_grid)
    tail_sums = jnp.flip(jnp.cumsum(jnp.flip(raised, 1), axis=1), 1)
    prompt_loss = jnp.sum(jnp.log(tail_sums) - rank_grid, axis=1)
    grid_grad = raised * jnp.cumsum(1.0 / tail_sums, axis=1) - 1.0
    return (jnp.mean(prompt_loss) / GROUP, grid_grad.reshape(-1)[response_slot])


def attend(query_states, key_states, value_states, allowed):
    count = query_states.shape[0]
    query_heads = query_states.reshape(count, KVH, H // KVH, HD)
    key_heads = key_states.reshape(-1, KVH, HD)
    value_heads = value_states.reshape(-1, KVH, HD)
    scores = jnp.einsum(
        "tkgd,ukd->kgtu", query_heads, key_heads, preferred_element_type=jnp.float32
    ) * HD ** (-0.5)
    weights = jnp.where(allowed, jnp.exp(scores), 0.0)
    totals = jnp.sum(weights, axis=-1, keepdims=True)
    soft_weights = (weights / totals).astype(jnp.bfloat16)
    attended = jnp.einsum(
        "kgtu,ukd->tkgd", soft_weights, value_heads, preferred_element_type=jnp.float32
    )
    return (soft_weights, attended)


def attend_backward(query_states, key_states, value_states, soft_weights, attended_heads, out_grad):
    count = query_states.shape[0]
    query_heads = query_states.reshape(count, KVH, H // KVH, HD)
    key_heads = key_states.reshape(-1, KVH, HD)
    value_heads = value_states.reshape(-1, KVH, HD)
    grad_heads = out_grad.reshape(count, KVH, H // KVH, HD)
    prob_grad = jnp.einsum(
        "tkgd,ukd->kgtu", grad_heads, value_heads, preferred_element_type=jnp.float32
    )
    row_delta = jnp.einsum("tkgd,tkgd->kgt", grad_heads.astype(jnp.float32), attended_heads)[
        ..., None
    ]
    score_grad = (soft_weights.astype(jnp.float32) * (prob_grad - row_delta) * HD ** (-0.5)).astype(
        jnp.bfloat16
    )
    query_grad = jnp.einsum(
        "kgtu,ukd->tkgd", score_grad, key_heads, preferred_element_type=jnp.float32
    )
    key_grad = jnp.einsum(
        "kgtu,tkgd->ukd", score_grad, query_heads, preferred_element_type=jnp.float32
    )
    value_grad = jnp.einsum(
        "kgtu,tkgd->ukd", soft_weights, grad_heads, preferred_element_type=jnp.float32
    )
    kv_terms = jnp.concatenate([key_grad.reshape(-1, KVD), value_grad.reshape(-1, KVD)], axis=1)
    return (query_grad.reshape(count, -1).astype(jnp.bfloat16), kv_terms)


def per_device(
    query_states, key_states, value_states, residual, norm_gain, reward_head, lengths, response_slot
):
    row_count = query_states.shape[0]
    reach = 1
    length_row = lengths[0]
    positions = lax.axis_index("seq") * row_count + jnp.arange(row_count, dtype=jnp.int32)
    query_doc = document_index(length_row, positions)
    key_list = [key_states]
    value_list = [value_states]
    position_list = [positions]
    distance = 1
    far_keys, far_values = passed_along((key_states, value_states), "seq", distance)
    key_list = [far_keys] + key_list
    value_list = [far_values] + value_list
    position_list = [positions - distance * row_count] + position_list
    near_keys = jnp.concatenate(key_list, axis=0)
    near_values = jnp.concatenate(value_list, axis=0)
    key_positions = jnp.concatenate(position_list, axis=0)
    key_doc = document_index(length_row, jnp.maximum(key_positions, 0))
    allowed = (
        (key_positions >= 0)[None, :]
        & (key_positions[None, :] <= positions[:, None])
        & (key_doc[None, :] == query_doc[:, None])
    )
    soft_weights, attended_heads = attend(query_states, near_keys, near_values, allowed)
    attended = attended_heads.reshape(row_count, -1)
    hidden = residual.astype(jnp.float32) + attended
    root_mean = jnp.sqrt(jnp.mean(hidden * hidden, axis=1, keepdims=True) + norm_eps)
    normed = hidden / root_mean
    scaled = normed * norm_gain
    token_score = jnp.dot(scaled, reward_head, precision=lax.Precision.HIGHEST)
    member = query_doc[None, :] == jnp.arange(DOCS, dtype=jnp.int32)[:, None]
    lengths_float = length_row.astype(jnp.float32)
    partial_reward = jnp.sum(jnp.where(member, token_score[None, :], 0.0), axis=1) / lengths_float
    doc_total = lax.psum(partial_reward, "seq")
    rewards = lax.all_gather(doc_total, "dp", axis=0, tiled=True)
    mean_loss, reward_grad = plackett(rewards, response_slot)
    own_grads = lax.dynamic_slice_in_dim(reward_grad, lax.axis_index("dp") * DOCS, DOCS)
    per_document = own_grads / lengths_float
    token_grad = jnp.sum(jnp.where(member, per_document[:, None], 0.0), axis=0)
    head_part = jnp.dot(token_grad, scaled, precision=lax.Precision.HIGHEST)
    gain_part = jnp.dot(token_grad, normed, precision=lax.Precision.HIGHEST)
    gain_total, head_grad = lax.psum((gain_part, head_part), ("dp", "seq"))
    gain_grad = reward_head * gain_total
    normed_grad = (loss_scale * token_grad)[:, None] * (reward_head * norm_gain)[None, :]
    hidden_grad = (
        normed_grad - normed * jnp.mean(normed_grad * normed, axis=1, keepdims=True)
    ) / root_mean
    out_grad = hidden_grad.astype(jnp.bfloat16)
    query_grad, kv_terms = attend_backward(
        query_states, near_keys, near_values, soft_weights, attended_heads, out_grad
    )
    local_term = lax.optimization_barrier(kv_terms[reach * row_count :].astype(jnp.bfloat16))
    kv_grad = local_term.astype(jnp.float32)
    distance = 1
    lower = (reach - distance) * row_count
    portion = kv_terms[lower : lower + row_count].astype(jnp.bfloat16)
    returned = passed_along(portion, "seq", -distance)
    kv_grad = kv_grad + returned.astype(jnp.float32)
    key_grad = kv_grad[:, :KVD].astype(jnp.bfloat16)
    value_grad = kv_grad[:, KVD:].astype(jnp.bfloat16)
    return (mean_loss, query_grad, key_grad, value_grad, gain_grad, head_grad)


def solution(mesh):
    return jax.shard_map(
        per_device,
        mesh=mesh,
        in_specs=(
            P(("dp", "seq"), None),
            P(("dp", "seq"), None),
            P(("dp", "seq"), None),
            P(("dp", "seq"), None),
            P(),
            P(),
            P("dp", None),
            P(),
        ),
        out_specs=(
            P(),
            P(("dp", "seq"), None),
            P(("dp", "seq"), None),
            P(("dp", "seq"), None),
            P(),
            P(),
        ),
        check_vma=False,
    )
```

profile of v0, /device:TPU:1, one launch (start us, length us, event | category | flops | bytes accessed | tf_op | source)
XLA Modules:
  0.0 914.8 jit_solution(4020982899964848864)
XLA Ops:
  0.6 16.4 %collective-permute-start = (bf16[128,1024]{1,0:T(8,128)(2,1)}, bf16[128,1024]{1,0:T(8,128)(2,1)S(1)}, u32[]{:S(2)}, u32[]{:S(2)}) collective-permute-start(bf16[128,1024]{1,0:T(8,128)(2,1)} %param.10), channel_id=1, source_target_pairs={{0,1},{1,2},{2,3},{4,5},{5,6},{6,7},{8,9},{9,10},{10,11},{12,13},{... | collective-permute-start | bytes 786440 | tf_op jit(solution)/shard_map/ppermute | solution.py:21
  17.0 1.1 copy.47
  18.2 1.9 collective-permute-start.1
  20.1 0.8 reduce-window.8
  21.0 0.1 convert_reduce_fusion.1
  21.1 0.1 convert_reduce_fusion
  21.1 0.2 compare_and_fusion
  21.3 0.7 compare_select_fusion
  22.0 1.6 copy.83
  23.7 1.3 dynamic-slice
  25.7 0.2 copy.46
  25.9 0.1 pad_maximum_fusion.1
  26.0 1.1 fusion.3
  27.2 0.9 divide_convert_fusion
  28.1 0.5 fusion.26
  28.6 0.9 copy-done
  29.4 2.0 copy.52
  31.5 2.4 multiply_reduce_fusion
  33.8 0.2 copy-done.4
  34.0 0.3 copy-done.8
  34.3 0.3 fusion.12
  34.6 0.4 copy-done.12
  35.0 0.0 copy-done.13
  35.0 1.7 fusion.13
  36.7 0.1 select_reduce_fusion.1
  36.9 11.8 %psum.21 = f32[8]{0:T(128)S(1)} all-reduce(f32[8]{0:T(128)S(1)} %bitcast_divide_fusion.1), channel_id=1, replica_groups=mesh['dp'=192,'seq'=4] {'seq'}, use_global_device_ids=true, to_apply=%region_6.7 | all-reduce | flops 8 | bytes 64 | tf_op jit(solution)/shard_map/psum | solution.py:119
  48.7 0.3 dynamic-update-slice
  49.0 618.4 %all-reduce = f32[1536]{0:T(1024)S(1)} all-reduce(f32[1536]{0:T(1024)S(1)} %dynamic-update-slice), channel_id=1, replica_groups=mesh['dp'=192,'seq'=4] {'dp'}, use_global_device_ids=true, to_apply=%add | all-reduce | flops 1536 | bytes 12288
  667.4 6.2 scatter_custom_fusion
  673.6 0.1 reshape.129
  673.7 0.1 rev.7
  673.8 0.2 reduce_window_sum.27
  674.0 0.1 rev.8
  674.1 0.6 broadcast_divide_fusion
  674.7 0.2 reduce_window_sum.28
  674.9 0.1 reduce_window_sum.29
  675.0 8.4 gather_fusion
  683.4 0.1 bitcast_divide_fusion
  683.5 0.1 select_reduce_fusion
  683.6 1.1 fusion.21
  684.6 1.2 fusion.8
  685.8 188.7 %all-reduce.1 = (f32[4096]{0:T(1024)S(1)}, f32[4096]{0:T(1024)}) all-reduce(f32[4096]{0:T(1024)S(1)} %bitcast.98, f32[4096]{0:T(1024)S(1)} %bitcast.99), channel_id=1, replica_groups=mesh['dp'=192,'seq'=4] {'dp','seq'}, use_global_device_ids=true, to_apply=%region_13.14 | all-reduce | flops 8192 | bytes 65536 | tf_op jit(solution)/shard_map/psum | solution.py:127
  874.5 0.6 fusion.25
  875.1 0.4 fusion.4
  875.5 0.4 fusion.6
  875.9 0.8 reshape.130
  876.7 1.0 copy.58
  877.7 2.0 bitcast_convert_fusion
  879.6 3.2 copy.72
  882.8 2.1 fusion.7
  884.9 0.1 copy-done.1
  885.0 1.6 fusion.28
  886.6 1.0 fusion.2
  887.6 1.2 copy.61
  888.9 2.0 fusion.27
  890.9 1.0 copy.60
  891.9 1.2 maximum_convert_fusion
  893.1 1.1 fusion.23
  894.2 2.6 collective-permute-start.2
  896.8 0.5 convolution_convert_fusion
  897.3 1.3 copy.62
  899.3 12.3 %collective-permute-done.2 = bf16[128,2048]{1,0:T(8,128)(2,1)} collective-permute-done((bf16[128,2048]{1,0:T(8,128)(2,1)}, bf16[128,2048]{1,0:T(8,128)(2,1)}, u32[]{:S(2)}, u32[]{:S(2)}) %collective-permute-start.2) | collective-permute-done | bytes 524320 | tf_op jit(solution)/shard_map/ppermute | solution.py:21
  911.5 1.3 add_convert_fusion
  912.9 0.8 fusion.24
  (39 shorter events, 0.2 us)
Async XLA Ops:
  0.6 25.0 %copy-start.11 = (bf16[128,1024]{1,0:T(8,128)(2,1)S(1)}, bf16[128,1024]{1,0:T(8,128)(2,1)}, u32[]{:S(2)}) copy-start(bf16[128,1024]{1,0:T(8,128)(2,1)} %param.10) | copy-start | bytes 786436
  0.6 25.0 %collective-permute-start = (bf16[128,1024]{1,0:T(8,128)(2,1)}, bf16[128,1024]{1,0:T(8,128)(2,1)S(1)}, u32[]{:S(2)}, u32[]{:S(2)}) collective-permute-start(bf16[128,1024]{1,0:T(8,128)(2,1)} %param.10), channel_id=1, source_target_pairs={{0,1},{1,2},{2,3},{4,5},{5,6},{6,7},{8,9},{9,10},{10,11},{12,13},{... | collective-permute-start | bytes 786440 | tf_op jit(solution)/shard_map/ppermute | solution.py:21
  18.2 7.8 collective-permute-start.1
  23.6 3.5 copy-start.7
  25.9 2.2 copy-start.5
  26.0 1.2 copy-start.9
  28.1 1.4 copy-start
  29.4 2.0 copy-start.2
  31.5 2.5 copy-start.4
  31.5 2.8 copy-start.8
  34.3 0.7 copy-start.12
  34.3 0.7 copy-start.13
  34.6 2.3 copy-start.14
  879.6 3.2 copy-start.3
  882.8 2.2 copy-start.1
  885.0 1.6 copy-start.6
  891.9 4.9 copy-start.10
  894.2 17.3 %collective-permute-start.2 = (bf16[128,2048]{1,0:T(8,128)(2,1)}, bf16[128,2048]{1,0:T(8,128)(2,1)}, u32[]{:S(2)}, u32[]{:S(2)}) collective-permute-start(bf16[128,2048]{1,0:T(8,128)(2,1)} %get-tuple-element.27), channel_id=1, source_target_pairs={{1,0},{2,1},{3,2},{5,4},{6,5},{7,6},{9,8},{10,9},{11,10},{13,12},{... | collective-permute-start | bytes 1572872 | tf_op jit(solution)/shard_map/ppermute | solution.py:21
where the time goes:
time: 926 us; the launch traced here: 915 us
  blocking collectives  819 us (88%)
  local copies, waits for them, and re-layouts  33.7 us (4%)
  starting transfers between devices  20.9 us (2%)
  other arithmetic  14.9 us (2%)
  waiting for transfers between devices  12.3 us (1%)
  matrix products  10.7 us (1%)
    unnamed x1, blocking collectives  618 us
    psum x1, blocking collectives, per_device(): gain_total, head_grad = lax.psum((gain_part, head_part), ('dp', 'seq'))  189 us
    ppermute x3, starting transfers between devices, passed_along(): return lax.ppermute(block, axis, route)  20.9 us
  transfers between devices with their start and end apart: 3, of which 1 were waited for; matrix products, arithmetic and copies ran while one was open for 1% of the time, Pallas kernels for 0%

commit v1 on v0

v1 whole, which is shorter than its diff:
```python
import functools
import jax
import jax.numpy as jnp
from jax import lax
from jax.experimental import pallas as pl
from jax.experimental.pallas import tpu as pltpu
from jax.sharding import Mesh, PartitionSpec as P

H = 32
KVH = 8
REP = 4
HD = 128
D = 4096
KVD = 1024
DOCS = 8
GROUP = 16
PROMPTS = 96
TOK = 128
LANES = 128
NY, NL, NX, NH, NC = 8, 6, 4, 2, 2
PLANE = ("y", "x", "c")
RING = ("l", "h")
N_PLANE = NY * NX * NC
N_RING = NL * NH
SLICES = NY * NX
PER = 11

loss_scale = 8192.0
norm_eps = 1e-05
LOG2E = 1.4426950408889634

NT = (((1,), (1,)), ((), ()))
NN = (((1,), (0,)), ((), ()))
TN = (((0,), (0,)), ((), ()))


def dot(a, b, dims):
    return lax.dot_general(a, b, dims, preferred_element_type=jnp.float32)


def block_of(g):
    return slice(g * HD, (g + 1) * HD)


def ends_of(len_ref):
    ends, total = [], 0
    for j in range(DOCS):
        total = total + len_ref[0, j]
        ends.append(total)
    return ends


def doc_of(pos, ends):
    doc = jnp.zeros(pos.shape, jnp.int32)
    for end in ends:
        doc = doc + jnp.where(pos >= end, 1, 0)
    return doc


def pick(index, values, like):
    out = jnp.zeros(index.shape, like)
    for j, value in enumerate(values):
        out = jnp.where(index == j, value, out)
    return out


def split3(x):
    one = x.astype(jnp.bfloat16)
    rest = x - one.astype(jnp.float32)
    two = rest.astype(jnp.bfloat16)
    three = (rest - two.astype(jnp.float32)).astype(jnp.bfloat16)
    return one, two, three


def stack_heads(ref, g):
    return jnp.concatenate([ref[:, block_of(REP * g + i)] for i in range(REP)], axis=0)


def forward_kernel(
    len_ref, q_ref, kh_ref, vh_ref, kl_ref, vl_ref, res_ref, gain_ref, head_ref,
    p_ref, u_ref, x_ref, hid_ref,
):
    seq = lax.axis_index("h") * NC + lax.axis_index("c")
    plane_at = lax.axis_index("y") * NX + lax.axis_index("x")
    ends = ends_of(len_ref)
    rows = lax.broadcasted_iota(jnp.int32, (TOK, TOK), 0)
    cols = lax.broadcasted_iota(jnp.int32, (TOK, TOK), 1)
    base = seq * TOK
    doc_r = doc_of(rows + base, ends)
    doc_c = doc_of(cols + base, ends)
    doc_h = jnp.where(seq > 0, doc_of(cols + base - TOK, ends), -1)
    mask_h = jnp.where(doc_r == doc_h, 1.0, 0.0)
    mask_l = jnp.where((doc_r == doc_c) & (cols <= rows), 1.0, 0.0)
    mask = jnp.concatenate([mask_h, mask_l], axis=1)
    mask = jnp.concatenate([mask] * REP, axis=0)
    squares = jnp.zeros((TOK, HD), jnp.float32)
    scored = jnp.zeros((TOK, HD), jnp.float32)
    for g in range(KVH):
        at = block_of(g)
        keys = jnp.concatenate([kh_ref[:, at], kl_ref[:, at]], axis=0)
        values = jnp.concatenate([vh_ref[:, at], vl_ref[:, at]], axis=0)
        scores = dot(stack_heads(q_ref, g), keys, NT)
        weights = jnp.exp2(scores * (HD ** (-0.5) * LOG2E)) * mask
        totals = jnp.sum(weights, axis=1, keepdims=True)
        soft = (weights * (1.0 / totals)).astype(jnp.bfloat16)
        p_ref[g] = soft
        out = dot(soft, values, NN)
        for i in range(REP):
            to = block_of(REP * g + i)
            hidden = res_ref[:, to].astype(jnp.float32) + out[i * TOK : (i + 1) * TOK]
            hid_ref[:, to] = hidden
            squares = squares + hidden * hidden
            scored = scored + hidden * (gain_ref[:, to] * head_ref[:, to])
    mean = jnp.sum(squares, axis=1, keepdims=True) * (1.0 / D)
    inverse = 1.0 / jnp.sqrt(mean + norm_eps)
    score = jnp.sum(scored, axis=1, keepdims=True) * inverse
    doc_col = doc_r[:, :1]
    lengths = [len_ref[0, j].astype(jnp.float32) for j in range(DOCS)]
    lane = lax.broadcasted_iota(jnp.int32, (1, LANES), 1)
    summed = jnp.sum(jnp.where(doc_r == (cols & 7), score, 0.0), axis=0, keepdims=True)
    reward = summed / pick(lane & 7, lengths, jnp.float32)
    row4 = lax.broadcasted_iota(jnp.int32, (4, LANES), 0)
    lane4 = lax.broadcasted_iota(jnp.int32, (4, LANES), 1)
    place = row4 * 16 + (lane4 >> 3)
    extra = jnp.where((place == plane_at) & (row4 < 2), reward, 0.0)
    x_ref[:, 4:8, :] = jnp.broadcast_to(extra[None], (N_PLANE, 4, LANES))
    doc16 = lax.broadcasted_iota(jnp.int32, (16, TOK), 0)
    member = jnp.where(doc16 == doc_of(cols[:16] + base, ends), 1.0, 0.0).astype(jnp.bfloat16)
    member = jnp.concatenate([member, member], axis=1)
    doc8 = lax.broadcasted_iota(jnp.int32, (8, 2 * LANES), 0)
    over = 1.0 / pick(doc8, lengths, jnp.float32)
    along = score * inverse * (1.0 / D)
    outer = inverse * loss_scale
    for t in range(D // 256):
        to = slice(t * 256, (t + 1) * 256)
        hidden = hid_ref[:, to]
        u_ref[:, to] = outer * (gain_ref[:, to] * head_ref[:, to] - hidden * along)
        normed = hidden * inverse
        high = normed.astype(jnp.bfloat16)
        low = (normed - high.astype(jnp.float32)).astype(jnp.bfloat16)
        sums = dot(member, jnp.concatenate([high, low], axis=0), NN)[:8] * over
        for s in range(2):
            part = sums[:, s * LANES : (s + 1) * LANES]
            x_ref[4 * t + 2 * s, 0:4, :] = part[0:4]
            x_ref[4 * t + 2 * s + 1, 0:4, :] = part[4:8]


def turn_kernel(r_ref, x_ref, sum_ref, flat_ref):
    got = r_ref[...].reshape(SLICES, NC, 8, LANES)
    both = got[:, 0] + got[:, 1]
    sum_ref[...] = both
    rewards = jnp.sum(both, axis=0)[4:6]
    stacked = jnp.concatenate([sum_ref[:, q, :] for q in range(4)], axis=0)
    flat_ref[0:LANES, :] = stacked.T
    flat_ref[LANES:, :] = jnp.zeros((8, LANES), jnp.float32)
    for a in range(N_RING):
        x_ref[a, 0:PER, :] = flat_ref[a * PER : (a + 1) * PER, :]
        x_ref[a, PER : PER + 2, :] = rewards
        x_ref[a, PER + 2 :, :] = jnp.zeros((16 - PER - 2, LANES), jnp.float32)


def backward_kernel(
    len_ref, slot_ref, r_ref, slot_all_ref, slot_half_ref, q_ref, kh_ref, vh_ref, kl_ref, vl_ref,
    p_ref, u_ref, qg_ref, back_ref, dk_ref, dv_ref, x_ref, loss_ref,
):
    low, high, core = lax.axis_index("l"), lax.axis_index("h"), lax.axis_index("c")
    seq = high * NC + core
    window = (lax.axis_index("y") * NL + low) * NX + lax.axis_index("x")
    ends = ends_of(len_ref)
    lower = lax.broadcasted_iota(jnp.int32, (PROMPTS, LANES), 0)
    rank = lax.broadcasted_iota(jnp.int32, (GROUP, LANES), 0)
    spread, onehot = [], []
    for at in range(NL):
        rewards = r_ref[2 * at, PER : PER + 2, :] + r_ref[2 * at + 1, PER : PER + 2, :]
        for half in range(2):
            slot = slot_all_ref[2 * at + half : 2 * at + half + 1, :]
            onehot.append(jnp.where(lower == (slot >> 4), 1.0, 0.0).astype(jnp.bfloat16))
            spread.append(jnp.where(rank == (slot & 15), rewards[half : half + 1], 0.0))
    pieces = jnp.concatenate(split3(jnp.concatenate(spread, axis=1)), axis=0)
    found = dot(pieces, jnp.concatenate(onehot, axis=1), NT)
    grid = found[0:16] + (found[16:32] + found[32:48])
    raised = jnp.exp(grid)
    tails = [raised[15:16]]
    for r in range(14, -1, -1):
        tails.insert(0, raised[r : r + 1] + tails[0])
    tail = jnp.concatenate(tails, axis=0)
    prompt_loss = jnp.sum(jnp.log(tail) - grid, axis=0, keepdims=True)
    loss_ref[0, 0] = jnp.sum(prompt_loss) * (1.0 / (PROMPTS * GROUP))
    inverse = 1.0 / tail
    runs = [inverse[0:1]]
    for r in range(1, 16):
        runs.append(runs[-1] + inverse[r : r + 1])
    grid_grad = raised * jnp.concatenate(runs, axis=0) - 1.0
    pieces = jnp.concatenate(split3(grid_grad), axis=0)
    picks, ranks = [], []
    for at in range(NL):
        slot = slot_half_ref[core, at : at + 1, :]
        picks.append(jnp.where(lower == (slot >> 4), 1.0, 0.0).astype(jnp.bfloat16))
        ranks.append(jnp.where(rank == (slot & 15), 1.0, 0.0))
    found = dot(pieces, jnp.concatenate(picks, axis=1), NN)
    found = (found[0:16] + (found[16:32] + found[32:48])) * jnp.concatenate(ranks, axis=1)
    doc_grad = jnp.sum(found, axis=0, keepdims=True)
    total = jnp.zeros((16, LANES), jnp.float32)
    for at in range(NL):
        both = r_ref[2 * at] + r_ref[2 * at + 1]
        total = total + both * doc_grad[:, at * LANES : (at + 1) * LANES]
    column = jnp.sum(total, axis=1, keepdims=True)
    row16 = lax.broadcasted_iota(jnp.int32, (16, LANES), 0)
    lane16 = lax.broadcasted_iota(jnp.int32, (16, LANES), 1)
    place = (low * NH + high) * PER + row16
    placed = jnp.where((lane16 == place) & (row16 < PER), column, 0.0)
    placed = jnp.sum(placed, axis=0, keepdims=True)
    x_ref[...] = jnp.broadcast_to(placed, (N_RING, LANES))
    rows = lax.broadcasted_iota(jnp.int32, (TOK, PROMPTS), 0)
    doc = doc_of(rows + seq * TOK, ends)
    slots = pick(doc, [slot_ref[window * DOCS + j] for j in range(DOCS)], jnp.int32)
    lanes = lax.broadcasted_iota(jnp.int32, (TOK, PROMPTS), 1)
    chosen = jnp.where(lanes == (slots >> 4), 1.0, 0.0).astype(jnp.bfloat16)
    found = dot(chosen, pieces, NT)
    lanes = lanes[:, :48]
    found = jnp.where((lanes & 15) == (slots[:, :48] & 15), found, 0.0)
    lengths = [len_ref[0, j].astype(jnp.float32) for j in range(DOCS)]
    token_grad = jnp.sum(found, axis=1, keepdims=True) / pick(doc[:, :1], lengths, jnp.float32)
    for g in range(KVH):
        at = block_of(g)
        keys = jnp.concatenate([kh_ref[:, at], kl_ref[:, at]], axis=0)
        values = jnp.concatenate([vh_ref[:, at], vl_ref[:, at]], axis=0)
        queries = stack_heads(q_ref, g)
        out_grad = jnp.concatenate(
            [(token_grad * u_ref[:, block_of(REP * g + i)]).astype(jnp.bfloat16) for i in range(REP)],
            axis=0,
        )
        soft = p_ref[g]
        prob_grad = dot(out_grad, values, NT)
        wide = soft.astype(jnp.float32)
        delta = jnp.sum(wide * prob_grad, axis=1, keepdims=True)
        score_grad = (wide * ((prob_grad - delta) * HD ** (-0.5))).astype(jnp.bfloat16)
        dk = dot(score_grad, queries, TN).astype(jnp.bfloat16)
        dv = dot(soft, out_grad, TN).astype(jnp.bfloat16)
        back_ref[:, at] = dk[:TOK]
        back_ref[:, KVD + g * HD : KVD + (g + 1) * HD] = dv[:TOK]
        dk_ref[:, at] = dk[TOK:]
        dv_ref[:, at] = dv[TOK:]
        dq = dot(score_grad, keys, NN).astype(jnp.bfloat16)
        for i in range(REP):
            qg_ref[:, block_of(REP * g + i)] = dq[i * TOK : (i + 1) * TOK]


VM = pl.BlockSpec(memory_space=pltpu.VMEM)
SM = pl.BlockSpec(memory_space=pltpu.SMEM)


def shape(dims, dtype):
    return jax.ShapeDtypeStruct(dims, dtype)


def cost(flops, moved):
    return pl.CostEstimate(flops=flops, bytes_accessed=moved, transcendentals=0)


def along_seq(block, distance):
    count = NH * NC
    route = [(i, i + distance) for i in range(count) if 0 <= i + distance < count]
    return lax.ppermute(block, ("h", "c"), route)


def exchange(block, axes):
    return lax.all_to_all(block, axes, 0, 0, tiled=True)


def per_device(
    query_states, key_states, value_states, residual, norm_gain, reward_head, lengths, response_slot
):
    bf, f32 = jnp.bfloat16, jnp.float32
    far_keys = along_seq(key_states, 1)
    far_values = along_seq(value_states, 1)
    slots = response_slot.reshape(NY, NL, NX, DOCS).transpose(1, 0, 2, 3).reshape(12, LANES)
    slot_half = response_slot.reshape(NY, NL, NX, 2, 4).transpose(3, 1, 4, 0, 2).reshape(2, NL, LANES)
    soft, unscaled, sums = pl.pallas_call(
        forward_kernel,
        in_specs=[SM] + [VM] * 8,
        out_specs=[VM] * 3,
        out_shape=[
            shape((KVH, REP * TOK, 2 * TOK), bf),
            shape((TOK, D), f32),
            shape((N_PLANE, 8, LANES), f32),
        ],
        scratch_shapes=[pltpu.VMEM((TOK, D), f32)],
        compiler_params=pltpu.CompilerParams(vmem_limit_bytes=24 * 1024 * 1024),
        cost_estimate=cost(540000000, 8000000),
        name="forward",
    )(
        lengths, query_states, far_keys, far_values, key_states, value_states, residual,
        norm_gain.reshape(1, D), reward_head.reshape(1, D),
    )
    sums = exchange(sums, PLANE)
    sums = pl.pallas_call(
        turn_kernel,
        in_specs=[VM],
        out_specs=VM,
        out_shape=shape((N_RING, 16, LANES), f32),
        scratch_shapes=[pltpu.VMEM((SLICES, 8, LANES), f32), pltpu.VMEM((LANES + 8, LANES), f32)],
        compiler_params=pltpu.CompilerParams(vmem_limit_bytes=8 * 1024 * 1024),
        name="turn",
    )(sums)
    sums = exchange(sums, RING)
    query_grad, back, key_part, value_part, total, loss = pl.pallas_call(
        backward_kernel,
        in_specs=[SM] * 2 + [VM] * 10,
        out_specs=[VM] * 5 + [SM],
        out_shape=[
            shape((TOK, D), bf),
            shape((TOK, 2 * KVD), bf),
            shape((TOK, KVD), bf),
            shape((TOK, KVD), bf),
            shape((N_RING, LANES), f32),
            shape((1, 1), f32),
        ],
        compiler_params=pltpu.CompilerParams(vmem_limit_bytes=24 * 1024 * 1024),
        cost_estimate=cost(1080000000, 9000000),
        name="backward",
    )(
        lengths, response_slot, sums, slots, slot_half, query_states, far_keys, far_values,
        key_states, value_states, soft, unscaled,
    )
    returned = along_seq(back, -1).astype(f32)
    total = exchange(total, RING)
    total = jnp.broadcast_to(jnp.sum(total, axis=0, keepdims=True), (N_PLANE, LANES))
    total = exchange(total, PLANE)
    total = jnp.sum(total.reshape(SLICES, NC, LANES), axis=1).reshape(D)
    key_grad = (key_part.astype(f32) + returned[:, :KVD]).astype(bf)
    value_grad = (value_part.astype(f32) + returned[:, KVD:]).astype(bf)
    return (
        loss.reshape(()), query_grad, key_grad, value_grad, reward_head * total, norm_gain * total
    )


def solution(mesh):
    axes = ("y", "l", "x", "h", "c")
    inner = Mesh(mesh.devices.reshape(NY, NL, NX, NH, NC), axes)
    dp, rows = ("y", "l", "x"), P(axes, None)
    return jax.shard_map(
        per_device,
        mesh=inner,
        in_specs=(rows, rows, rows, rows, P(), P(), P(dp, None), P()),
        out_specs=(P(), rows, rows, rows, P(), P()),
        check_vma=False,
    )
```

time: 926 us -> 149 us (0.16); the launches traced: 915 us -> 148 us
  blocking collectives: 819 us -> 59.9 us
  starting transfers between devices: 20.9 us -> 44.9 us
  other arithmetic: 14.9 us -> 2.75 us
  Pallas kernels: 0 us -> 10.8 us
  matrix products: 10.7 us -> 0 us
  local copies, waits for them, and re-layouts: 33.7 us -> 23.4 us
    unnamed x1 -> x0, blocking collectives: 618 us -> none
    psum x2 -> x0, blocking collectives: 201 us -> none  [the longest x1 189 us: per_device(): gain_total, head_grad = lax.psum((gain_part, head_part), ('dp', 'seq'))]
    all_to_all x0 -> x3, blocking collectives: none -> 59.9 us  [exchange(): return lax.all_to_all(block, axes, 0, 0, tiled=True)]
    all_to_all x0 -> x1, starting transfers between devices: none -> 21.8 us  [exchange(): return lax.all_to_all(block, axes, 0, 0, tiled=True)]
    pallas_call x0 -> x3, Pallas kernels: none -> 10.8 us  [the longest x1 6.93 us: per_device(): pl.pallas_call(backward_kernel, in_specs=[SM] * 2 + [VM] * 10, out_specs=...]
    dot_general x9 -> x0, matrix products: 10.7 us -> none  [the longest x1 2.03 us: attend_backward(): jnp.einsum('kgtu,tkgd->ukd', score_grad, query_heads, preferred_element_t...]
  transfers between devices with their start and end apart: 3 -> 4, of which waited for: 1 -> 3; matrix products, arithmetic and copies ran while one was open for 1% -> 6% of each run, Pallas kernels for 0% -> 0%
where the time goes in v1:
time: 149 us; the launch traced here: 148 us
  blocking collectives  59.9 us (40%)
  starting transfers between devices  44.9 us (30%)
  local copies, waits for them, and re-layouts  23.4 us (16%)
  Pallas kernels  10.8 us (7%)
  waiting for transfers between devices  5.55 us (4%)
  other arithmetic  2.75 us (2%)
    all_to_all x3, blocking collectives, exchange(): return lax.all_to_all(block, axes, 0, 0, tiled=True)  59.9 us
    ppermute x3, starting transfers between devices, along_seq(): return lax.ppermute(block, ('h', 'c'), route)  23 us
    all_to_all x1, starting transfers between devices, exchange(): return lax.all_to_all(block, axes, 0, 0, tiled=True)  21.8 us
    unnamed x46, local copies, waits for them, and re-layouts  15.1 us
    pallas_call x1, Pallas kernels, per_device(): pl.pallas_call(backward_kernel, in_specs=[SM] * 2 + [VM] * 10, out_specs=...  6.93 us
    ppermute x3, waiting for transfers between devices, along_seq(): return lax.ppermute(block, ('h', 'c'), route)  4.49 us
    reshape x3, local copies, waits for them, and re-layouts, per_device(): response_slot.reshape(NY, NL, NX, 2, 4).transpose(3, 1, 4, 0, 2)  4.36 us
    pallas_call x1, Pallas kernels, per_device(): pl.pallas_call(forward_kernel, in_specs=[SM] + [VM] * 8, out_specs=[VM] *...  3.1 us
  transfers between devices with their start and end apart: 4, of which 3 were waited for; matrix products, arithmetic and copies ran while one was open for 6% of the time, Pallas kernels for 0%

profile of v1, /device:TPU:1, one launch (start us, length us, event | category | flops | bytes accessed | tf_op | source)
XLA Modules:
  0.0 148.1 jit_solution(2486986118771421918)
XLA Ops:
  0.6 16.2 %collective-permute-start = (bf16[128,1024]{1,0:T(8,128)(2,1)}, bf16[128,1024]{1,0:T(8,128)(2,1)S(1)}, u32[]{:S(2)}, u32[]{:S(2)}) collective-permute-start(bf16[128,1024]{1,0:T(8,128)(2,1)} %kl_ref.3), channel_id=1, source_target_pairs={{0,1},{1,2},{2,3},{4,5},{5,6},{6,7},{8,9},{9,10},{10,11},{12,13},{... | collective-permute-start | bytes 786440 | tf_op jit(solution)/shard_map/ppermute | solution.py:264
  16.9 1.9 %collective-permute-start.1 = (bf16[128,1024]{1,0:T(8,128)(2,1)}, bf16[128,1024]{1,0:T(8,128)(2,1)S(1)}, u32[]{:S(2)}, u32[]{:S(2)}) collective-permute-start(bf16[128,1024]{1,0:T(8,128)(2,1)} %vl_ref.3), channel_id=1, source_target_pairs={{0,1},{1,2},{2,3},{4,5},{5,6},{6,7},{8,9},{9,10},{10,11},{12,13},{... | collective-permute-start | bytes 786440 | tf_op jit(solution)/shard_map/ppermute | solution.py:264
  18.8 1.7 %collective-permute-done.kh_ref = bf16[128,1024]{1,0:T(8,128)(2,1)S(1)} collective-permute-done((bf16[128,1024]{1,0:T(8,128)(2,1)}, bf16[128,1024]{1,0:T(8,128)(2,1)S(1)}, u32[]{:S(2)}, u32[]{:S(2)}) %collective-permute-start) | collective-permute-done | bytes 262176 | tf_op jit(solution)/shard_map/ppermute | solution.py:264
  20.5 0.0 copy-start.9
  20.5 2.8 %collective-permute-done.1.vh_ref = bf16[128,1024]{1,0:T(8,128)(2,1)S(1)} collective-permute-done((bf16[128,1024]{1,0:T(8,128)(2,1)}, bf16[128,1024]{1,0:T(8,128)(2,1)S(1)}, u32[]{:S(2)}, u32[]{:S(2)}) %collective-permute-start.1) | collective-permute-done | bytes 262176 | tf_op jit(solution)/shard_map/ppermute | solution.py:264
  23.3 0.0 copy-start.11
  23.3 0.0 copy-start
  23.3 1.3 copy-done
  24.6 0.0 copy-start.4
  24.6 1.2 copy-done.4
  25.9 0.0 copy-start.5
  25.9 0.9 copy-done.5
  26.8 0.0 copy-start.7
  26.8 0.9 copy-done.7
  27.8 0.0 copy-start.16
  27.8 0.7 copy-done.16
  28.5 0.0 copy-start.18
  28.5 0.7 copy-done.18
  29.2 0.0 copy-start.21
  29.2 0.7 copy-done.21
  29.8 0.0 copy-start.1
  29.9 0.0 copy-start.6
  29.9 3.1 %forward.1 = (bf16[8,512,256]{2,1,0:T(8,128)(2,1)S(1)}, f32[128,4096]{1,0:T(8,128)S(1)}, f32[64,8,128]{2,1,0:T(8,128)S(1)}) custom-call(s32[1,8]{1,0:T(1,128)S(1)} %copy-done.21, bf16[128,4096]{1,0:T(8,128)(2,1)S(1)} %copy-done, bf16[128,1024]{1,0:T(8,128)(2,1)S(1)} %collective-permute-done.kh_ref, bf16[128,1024]{1,0:T(8,128)(2,1)S(1)} %collective-permute-done.1.vh_ref, ...), custom_call_target="tpu_custom_call" | custom-call | flops 540000000 | bytes 8000000 | tf_op jit(solution)/shard_map/forward/pallas_call | solution.py:279
  33.0 0.0 copy-done.9
  33.0 0.0 copy-start.2
  33.0 1.3 copy-done.2
  34.3 0.0 copy-done.11
  34.3 23.2 %all_to_all.25.r_ref = f32[64,8,128]{2,1,0:T(8,128)S(1)} all-to-all(f32[64,8,128]{2,1,0:T(8,128)S(1)} %get-tuple-element.15), channel_id=1, replica_groups=mesh['y'=8,'l'=6,'x'=4,'h'=2,'c'=2] {'y','x','c'}, dimensions={0} | all-to-all | bytes 524288 | tf_op jit(solution)/shard_map/all_to_all | solution.py:268
  57.5 0.8 turn.1
  58.3 21.8 %all-to-all-start.1 = ((f32[12,16,128]{2,1,0:T(8,128)}), f32[12,16,128]{2,1,0:T(8,128)S(1)}, u32[]{:S(2)}, u32[]{:S(2)}) async-start(f32[12,16,128]{2,1,0:T(8,128)} %turn.1), calls=%async_computation.1 | async-start | bytes 196608 | tf_op jit(solution)/shard_map/all_to_all | solution.py:268
  80.1 0.0 copy-done.15
  80.1 0.8 reshape.50
  80.9 1.0 reshape.52
  81.9 1.5 %copy.30 = s32[6,8,4,8]{3,2,1,0:T(4,128)} copy(s32[6,8,4,8]{3,2,0,1:T(4,128)} %bitcast.16) | data formatting | bytes 12288 | tf_op jit(solution)/shard_map/transpose | solution.py:277
  83.5 1.6 %reshape.51.slot_all_ref = s32[12,128]{1,0:T(8,128)} reshape(s32[6,8,4,8]{3,2,1,0:T(4,128)} %copy.30) | data formatting | bytes 12288 | tf_op jit(solution)/shard_map/reshape | solution.py:277
  85.1 2.3 %copy.35 = s32[2,6,4,8,4]{4,3,2,1,0:T(8,128)} copy(s32[2,6,4,8,4]{2,0,4,1,3:T(2,128)} %bitcast.15) | data formatting | bytes 12288 | tf_op jit(solution)/shard_map/reshape | solution.py:278
  87.4 1.1 reshape.57.slot_half_ref
  88.5 1.1 all-to-all-done.1.r_ref
  89.5 0.0 copy-done.1
  89.5 0.0 copy-done.6
  89.5 0.0 copy-start.3
  89.5 1.6 %copy-done.3 = f32[128,4096]{1,0:T(8,128)S(1)} copy-done((f32[128,4096]{1,0:T(8,128)S(1)}, f32[128,4096]{1,0:T(8,128)}, u32[]{:S(2)}) %copy-start.3) | copy-done | bytes 2097176
  91.1 0.0 copy-start.8
  91.1 0.9 copy-done.8
  92.1 0.0 copy-start.10
  92.1 0.9 copy-done.10
  93.0 0.0 copy-start.12
  93.0 0.9 copy-done.12
  94.0 0.0 copy-start.20
  94.0 0.7 copy-done.20
  94.7 0.7 copy-done.22
  95.3 6.9 %backward.1 = (bf16[128,4096]{1,0:T(8,128)(2,1)}, bf16[128,2048]{1,0:T(8,128)(2,1)}, bf16[128,1024]{1,0:T(8,128)(2,1)S(1)}, bf16[128,1024]{1,0:T(8,128)(2,1)S(1)...) custom-call(s32[1,8]{1,0:T(1,128)S(1)} %copy-done.22, s32[1536]{0:T(1024)S(1)} %copy-done.15, ...), custom_call_target="tpu_custom_call" | custom-call | flops 1080000000 | bytes 9000000 | tf_op jit(solution)/shard_map/backward/pallas_call | solution.py:307
  102.3 0.0 copy-start.13
  102.3 0.7 copy-done.13
  103.0 0.7 copy-done.14
  103.7 4.9 %collective-permute-start.2 = (bf16[128,2048]{1,0:T(8,128)(2,1)}, bf16[128,2048]{1,0:T(8,128)(2,1)S(1)}, u32[]{:S(2)}, u32[]{:S(2)}) collective-permute-start(bf16[128,2048]{1,0:T(8,128)(2,1)} %get-tuple-element.21), channel_id=1, source_target_pairs={{1,0},{2,1},{3,2},{5,4},{6,5},{7,6},{9,8},{10,9},{11,10},{13,12},{... | collective-permute-start | bytes 1572872 | tf_op jit(solution)/shard_map/ppermute | solution.py:264
  108.6 17.2 %all_to_all.26 = f32[12,1,128]{2,1,0:T(1,128)S(1)} all-to-all(f32[12,1,128]{2,1,0:T(1,128)S(1)} %copy.33), channel_id=1, replica_groups=mesh['y'=8,'l'=6,'x'=4,'h'=2,'c'=2] {'l','h'}, dimensions={0} | all-to-all | bytes 12288 | tf_op jit(solution)/shard_map/all_to_all | solution.py:268
  125.8 19.6 %all_to_all.27 = f32[64,1,128]{2,1,0:T(1,128)S(1)} all-to-all(f32[64,1,128]{2,1,0:T(1,128)S(1)} %broadcast_in_dim.2), channel_id=1, replica_groups=mesh['y'=8,'l'=6,'x'=4,'h'=2,'c'=2] {'y','x','c'}, dimensions={0} | all-to-all | bytes 65536 | tf_op jit(solution)/shard_map/all_to_all | solution.py:268
  145.4 0.0 copy-done.17
  145.4 0.0 copy-done.19
  145.5 0.6 bitcast_multiply_fusion
  146.1 0.0 collective-permute-done.2
  146.1 0.1 convert_element_type.16
  146.2 2.0 %fusion = (bf16[128,1024]{1,0:T(8,128)(2,1)}, bf16[128,1024]{1,0:T(8,128)(2,1)}) fusion(f32[128,2048]{1,0:T(8,128)S(1)} %convert_element_type.16, bf16[128,1024]{1,0:T(8,128)(2,1)} %copy-done.14, bf16[128,1024]{1,0:T(8,128)(2,1)} %copy-done.13), kind=kLoop, calls=%fused_computation.1 | loop fusion | flops 786432 | bytes 2097152 | tf_op jit(solution)/shard_map/convert_element_type | solution.py:332
  (9 shorter events, 0.1 us)
Async XLA Ops:
  0.6 19.9 %collective-permute-start = (bf16[128,1024]{1,0:T(8,128)(2,1)}, bf16[128,1024]{1,0:T(8,128)(2,1)S(1)}, u32[]{:S(2)}, u32[]{:S(2)}) collective-permute-start(bf16[128,1024]{1,0:T(8,128)(2,1)} %kl_ref.3), channel_id=1, source_target_pairs={{0,1},{1,2},{2,3},{4,5},{5,6},{6,7},{8,9},{9,10},{10,11},{12,13},{... | collective-permute-start | bytes 786440 | tf_op jit(solution)/shard_map/ppermute | solution.py:264
  16.9 6.4 %collective-permute-start.1 = (bf16[128,1024]{1,0:T(8,128)(2,1)}, bf16[128,1024]{1,0:T(8,128)(2,1)S(1)}, u32[]{:S(2)}, u32[]{:S(2)}) collective-permute-start(bf16[128,1024]{1,0:T(8,128)(2,1)} %vl_ref.3), channel_id=1, source_target_pairs={{0,1},{1,2},{2,3},{4,5},{5,6},{6,7},{8,9},{9,10},{10,11},{12,13},{... | collective-permute-start | bytes 786440 | tf_op jit(solution)/shard_map/ppermute | solution.py:264
  20.5 12.5 %copy-start.9 = (bf16[128,1024]{1,0:T(8,128)(2,1)}, bf16[128,1024]{1,0:T(8,128)(2,1)S(1)}, u32[]{:S(2)}) copy-start(bf16[128,1024]{1,0:T(8,128)(2,1)S(1)} %collective-permute-done.kh_ref) | copy-start | bytes 786436
  23.3 11.0 %copy-start.11 = (bf16[128,1024]{1,0:T(8,128)(2,1)}, bf16[128,1024]{1,0:T(8,128)(2,1)S(1)}, u32[]{:S(2)}) copy-start(bf16[128,1024]{1,0:T(8,128)(2,1)S(1)} %collective-permute-done.1.vh_ref) | copy-start | bytes 786436
  23.3 1.3 copy-start
  24.6 1.2 copy-start.4
  25.9 0.9 copy-start.5
  26.8 0.9 copy-start.7
  27.8 0.7 copy-start.16
  28.5 0.7 copy-start.18
  29.2 0.7 copy-start.21
  29.8 50.3 %copy-start.15 = (s32[1536]{0:T(1024)S(1)}, s32[1536]{0:T(1024)}, u32[]{:S(2)}) copy-start(s32[1536]{0:T(1024)} %slot_ref.1) | copy-start | bytes 18436
  29.8 59.7 %copy-start.1 = (bf16[128,4096]{1,0:T(8,128)(2,1)S(1)}, bf16[128,4096]{1,0:T(8,128)(2,1)}, u32[]{:S(2)}) copy-start(bf16[128,4096]{1,0:T(8,128)(2,1)} %q_ref.3) | copy-start | bytes 3145732
  29.9 59.7 %copy-start.6 = (bf16[128,1024]{1,0:T(8,128)(2,1)S(1)}, bf16[128,1024]{1,0:T(8,128)(2,1)}, u32[]{:S(2)}) copy-start(bf16[128,1024]{1,0:T(8,128)(2,1)} %kl_ref.3) | copy-start | bytes 786436
  33.0 1.3 copy-start.2
  58.3 31.3 %all-to-all-start.1 = ((f32[12,16,128]{2,1,0:T(8,128)}), f32[12,16,128]{2,1,0:T(8,128)S(1)}, u32[]{:S(2)}, u32[]{:S(2)}) async-start(f32[12,16,128]{2,1,0:T(8,128)} %turn.1), calls=%async_computation.1 | async-start | bytes 196608 | tf_op jit(solution)/shard_map/all_to_all | solution.py:268
  89.5 1.6 %copy-start.3 = (f32[128,4096]{1,0:T(8,128)S(1)}, f32[128,4096]{1,0:T(8,128)}, u32[]{:S(2)}) copy-start(f32[128,4096]{1,0:T(8,128)} %copy-done.2) | copy-start | bytes 6291460
  91.1 0.9 copy-start.8
  92.1 0.9 copy-start.10
  93.0 0.9 copy-start.12
  94.0 0.7 copy-start.20
  94.7 0.7 copy-start.22
  95.3 50.1 %copy-start.17 = (f32[4096]{0:T(1024)S(1)}, f32[4096]{0:T(1024)}, u32[]{:S(2)}) copy-start(f32[4096]{0:T(1024)} %param.12) | copy-start | bytes 49156
  95.3 50.1 %copy-start.19 = (f32[4096]{0:T(1024)S(1)}, f32[4096]{0:T(1024)}, u32[]{:S(2)}) copy-start(f32[4096]{0:T(1024)} %param.13) | copy-start | bytes 49156
  102.3 0.7 copy-start.13
  103.0 0.7 copy-start.14
  103.7 42.4 %collective-permute-start.2 = (bf16[128,2048]{1,0:T(8,128)(2,1)}, bf16[128,2048]{1,0:T(8,128)(2,1)S(1)}, u32[]{:S(2)}, u32[]{:S(2)}) collective-permute-start(bf16[128,2048]{1,0:T(8,128)(2,1)} %get-tuple-element.21), channel_id=1, source_target_pairs={{1,0},{2,1},{3,2},{5,4},{6,5},{7,6},{9,8},{10,9},{11,10},{13,12},{... | collective-permute-start | bytes 1572872 | tf_op jit(solution)/shard_map/ppermute | solution.py:264

commit v2 on v1

v2 whole, which is shorter than its diff:
```python
import jax
import jax.numpy as jnp
from jax import lax
from jax.experimental import pallas as pl
from jax.experimental.pallas import tpu as pltpu
from jax.sharding import Mesh, PartitionSpec as P

H = 32
KVH = 8
REP = 4
HD = 128
D = 4096
KVD = 1024
DOCS = 8
GROUP = 16
PROMPTS = 96
TOK = 128
LANES = 128
NY, NL, NX, NH, NC = 8, 6, 4, 2, 2
PLANE = ("y", "x", "c")
RING = ("l", "h")
N_PLANE = NY * NX * NC
N_RING = NL * NH
COLUMNS = NY * NX
WIDE = 384
PER = 3

loss_scale = 8192.0
norm_eps = 1e-05
LOG2E = 1.4426950408889634

NT = (((1,), (1,)), ((), ()))
NN = (((1,), (0,)), ((), ()))
TN = (((0,), (0,)), ((), ()))


def dot(a, b, dims):
    return lax.dot_general(a, b, dims, preferred_element_type=jnp.float32)


def block_of(g):
    return slice(g * HD, (g + 1) * HD)


def ends_of(len_ref):
    ends, total = [], 0
    for j in range(DOCS):
        total = total + len_ref[0, j]
        ends.append(total)
    return ends


def doc_of(pos, ends):
    doc = jnp.zeros(pos.shape, jnp.int32)
    for end in ends:
        doc = doc + jnp.where(pos >= end, 1, 0)
    return doc


def pick(index, values, like):
    out = jnp.zeros(index.shape, like)
    for j, value in enumerate(values):
        out = jnp.where(index == j, value, out)
    return out


def split3(x):
    one = x.astype(jnp.bfloat16)
    rest = x - one.astype(jnp.float32)
    two = rest.astype(jnp.bfloat16)
    three = (rest - two.astype(jnp.float32)).astype(jnp.bfloat16)
    return one, two, three


def stack_heads(ref, g):
    return jnp.concatenate([ref[:, block_of(REP * g + i)] for i in range(REP)], axis=0)


def start_all(pairs, sems):
    copies = [pltpu.make_async_copy(src, dst, sems.at[i]) for i, (src, dst) in enumerate(pairs)]
    for copy in copies:
        copy.start()
    return copies


def window_place():
    seq = lax.axis_index("h") * NC + lax.axis_index("c")
    window = (lax.axis_index("y") * NL + lax.axis_index("l")) * NX + lax.axis_index("x")
    return seq, window


def weigh(queries, keys, mask):
    scores = dot(queries, keys, NT)
    return jnp.exp2(scores * (HD ** (-0.5) * LOG2E)) * mask


def local_kernel(
    len_ref, q_hbm, kl_hbm, vl_hbm, res_hbm, q_ref, kl_ref, vl_ref, res_ref, w_ref, sems
):
    copies = start_all([(kl_hbm, kl_ref), (q_hbm, q_ref), (vl_hbm, vl_ref), (res_hbm, res_ref)], sems)
    seq, _ = window_place()
    ends = ends_of(len_ref)
    rows = lax.broadcasted_iota(jnp.int32, (TOK, TOK), 0)
    cols = lax.broadcasted_iota(jnp.int32, (TOK, TOK), 1)
    base = seq * TOK
    same = doc_of(rows + base, ends) == doc_of(cols + base, ends)
    mask = jnp.where(same & (cols <= rows), 1.0, 0.0)
    mask = jnp.concatenate([mask] * REP, axis=0)
    copies[0].wait()
    copies[1].wait()
    for g in range(KVH):
        w_ref[g] = weigh(stack_heads(q_ref, g), kl_ref[:, block_of(g)], mask)
    copies[2].wait()
    copies[3].wait()


def forward_kernel(
    len_ref, slot_ref, q_ref, kh_ref, vh_ref, vl_ref, res_ref, w_ref, gain_ref, head_ref,
    p_ref, u_ref, x_ref, hid_ref,
):
    seq, window = window_place()
    ends = ends_of(len_ref)
    rows = lax.broadcasted_iota(jnp.int32, (TOK, TOK), 0)
    cols = lax.broadcasted_iota(jnp.int32, (TOK, TOK), 1)
    base = seq * TOK
    doc_r = doc_of(rows + base, ends)
    doc_h = jnp.where(seq > 0, doc_of(cols + base - TOK, ends), -1)
    mask = jnp.where(doc_r == doc_h, 1.0, 0.0)
    mask = jnp.concatenate([mask] * REP, axis=0)
    squares = jnp.zeros((TOK, HD), jnp.float32)
    scored = jnp.zeros((TOK, HD), jnp.float32)
    for g in range(KVH):
        at = block_of(g)
        values = jnp.concatenate([vh_ref[:, at], vl_ref[:, at]], axis=0)
        weights = jnp.concatenate(
            [weigh(stack_heads(q_ref, g), kh_ref[:, at], mask), w_ref[g]], axis=1
        )
        totals = jnp.sum(weights, axis=1, keepdims=True)
        soft = (weights * (1.0 / totals)).astype(jnp.bfloat16)
        p_ref[g] = soft
        out = dot(soft, values, NN)
        for i in range(REP):
            to = block_of(REP * g + i)
            hidden = res_ref[:, to].astype(jnp.float32) + out[i * TOK : (i + 1) * TOK]
            hid_ref[:, to] = hidden
            squares = squares + hidden * hidden
            scored = scored + hidden * (gain_ref[:, to] * head_ref[:, to])
    mean = jnp.sum(squares, axis=1, keepdims=True) * (1.0 / D)
    inverse = 1.0 / jnp.sqrt(mean + norm_eps)
    score = jnp.sum(scored, axis=1, keepdims=True) * inverse
    lengths = [len_ref[0, j].astype(jnp.float32) for j in range(DOCS)]
    doc8 = lax.broadcasted_iota(jnp.int32, (DOCS, LANES), 0)
    lane8 = lax.broadcasted_iota(jnp.int32, (DOCS, LANES), 1)
    over = 1.0 / pick(doc8, lengths, jnp.float32)
    by_lane = jnp.sum(jnp.where(doc_r == cols, score, 0.0), axis=0, keepdims=True)
    reward = jnp.sum(jnp.where(lane8 == doc8, by_lane, 0.0), axis=1, keepdims=True) * over
    slots = pick(doc8, [slot_ref[window * DOCS + j] for j in range(DOCS)], jnp.int32)
    slots = jnp.where(seq == 0, slots.astype(jnp.float32), 0.0)
    extra = jnp.where(lane8 < 64, reward, slots)
    for a in range(N_RING):
        x_ref[a, :, WIDE:] = extra
    empty = jnp.zeros((DOCS, LANES), jnp.float32)
    for tile in range(D // LANES, N_RING * 3):
        x_ref[tile // 3, :, (tile % 3) * LANES : (tile % 3 + 1) * LANES] = empty
    doc16 = lax.broadcasted_iota(jnp.int32, (16, TOK), 0)
    member = jnp.where(doc16 == doc_of(cols[:16] + base, ends), 1.0, 0.0).astype(jnp.bfloat16)
    member = jnp.concatenate([member, member], axis=1)
    along = score * inverse * (1.0 / D)
    outer = inverse * loss_scale
    for t in range(D // 256):
        to = slice(t * 256, (t + 1) * 256)
        hidden = hid_ref[:, to]
        u_ref[:, to] = outer * (gain_ref[:, to] * head_ref[:, to] - hidden * along)
        normed = hidden * inverse
        high = normed.astype(jnp.bfloat16)
        low = (normed - high.astype(jnp.float32)).astype(jnp.bfloat16)
        sums = dot(member, jnp.concatenate([high, low], axis=0), NN)[:DOCS]
        for s in range(2):
            tile = 2 * t + s
            x_ref[tile // 3, :, (tile % 3) * LANES : (tile % 3 + 1) * LANES] = (
                sums[:, s * LANES : (s + 1) * LANES] * over
            )


def turn_kernel(r_ref, x_ref, flat_ref):
    got = r_ref[...].reshape(NL, NH, DOCS, WIDE + LANES)
    docs = (got[:, 0] + got[:, 1]).reshape(NL * DOCS, WIDE + LANES)
    docs = jnp.concatenate([docs, jnp.zeros((64 - NL * DOCS, WIDE + LANES), jnp.float32)], axis=0)
    empty = jnp.zeros_like(docs)
    first = jnp.concatenate([docs, empty], axis=0).T
    second = jnp.concatenate([empty, docs], axis=0).T
    flat_ref[...] = first[: WIDE // 2] + second[WIDE // 2 : WIDE]
    extra = first[WIDE : WIDE + 1] + second[WIDE + 64 : WIDE + 65]
    for b in range(N_PLANE):
        x_ref[b, 0:PER, :] = flat_ref[b * PER : (b + 1) * PER, :]
        x_ref[b, PER : PER + 1, :] = extra


def backward_kernel(
    len_ref, slot_ref, r_ref, q_ref, kh_ref, vh_ref, kl_ref, vl_ref, p_ref, u_ref,
    qg_hbm, back_ref, dk_ref, dv_ref, x_ref, loss_ref,
    qg_ref, sum_ref, out_sems,
):
    core = lax.axis_index("c")
    seq, window = window_place()
    plane_at = (lax.axis_index("y") * NX + lax.axis_index("x")) * NC + core
    ends = ends_of(len_ref)
    got = r_ref[...].reshape(COLUMNS, NC, PER + 1, LANES)
    sum_ref[...] = got[:, 0] + got[:, 1]
    extra = sum_ref[:, PER, :]
    lane32 = lax.broadcasted_iota(jnp.int32, (COLUMNS, LANES), 1)
    slots = jnp.where(lane32 < 64, pltpu.roll(extra, 64, 1), extra).astype(jnp.int32)
    rewards = jnp.where(lane32 < 64, extra, 0.0)
    lower = lax.broadcasted_iota(jnp.int32, (PROMPTS, LANES), 0)
    rank = lax.broadcasted_iota(jnp.int32, (GROUP, LANES), 0)
    spread, onehot, ranked = [], [], []
    for at in range(COLUMNS):
        slot = slots[at : at + 1]
        onehot.append(jnp.where(lower == (slot >> 4), 1.0, 0.0).astype(jnp.bfloat16))
        same = rank == (slot & 15)
        ranked.append(jnp.where(same, 1.0, 0.0))
        spread.append(jnp.where(same, rewards[at : at + 1], 0.0))
    onehot = jnp.concatenate(onehot, axis=1)
    pieces = jnp.concatenate(split3(jnp.concatenate(spread, axis=1)), axis=0)
    found = dot(pieces, onehot, NT)
    grid = found[0:16] + (found[16:32] + found[32:48])
    raised = jnp.exp(grid)
    tails = [raised[15:16]]
    for r in range(14, -1, -1):
        tails.insert(0, raised[r : r + 1] + tails[0])
    tail = jnp.concatenate(tails, axis=0)
    prompt_loss = jnp.sum(jnp.log(tail) - grid, axis=0, keepdims=True)
    loss_ref[0, 0] = jnp.sum(prompt_loss) * (1.0 / (PROMPTS * GROUP))
    inverse = 1.0 / tail
    runs = [inverse[0:1]]
    for r in range(1, 16):
        runs.append(runs[-1] + inverse[r : r + 1])
    grid_grad = raised * jnp.concatenate(runs, axis=0) - 1.0
    pieces = jnp.concatenate(split3(grid_grad), axis=0)
    found = dot(pieces, onehot, NN)
    total = jnp.zeros((PER + 1, LANES), jnp.float32)
    for at in range(COLUMNS):
        part = found[:, at * LANES : (at + 1) * LANES]
        part = (part[0:16] + (part[16:32] + part[32:48])) * ranked[at]
        total = total + sum_ref[at] * jnp.sum(part, axis=0, keepdims=True)
    row = lax.broadcasted_iota(jnp.int32, (PER + 1, LANES), 0)
    lane = lax.broadcasted_iota(jnp.int32, (PER + 1, LANES), 1)
    first = jnp.sum(jnp.where(lane < 64, total, 0.0), axis=1, keepdims=True)
    second = jnp.sum(jnp.where(lane < 64, 0.0, total), axis=1, keepdims=True)
    feature = row * LANES + lane
    placed = jnp.zeros((PER + 1, LANES), jnp.float32)
    for i in range(PER):
        to = plane_at * PER + i
        placed = jnp.where(feature == to, first[i : i + 1], placed)
        placed = jnp.where(feature == to + WIDE // 2, second[i : i + 1], placed)
    x_ref[...] = jnp.broadcast_to(placed[None], (N_PLANE, PER + 1, LANES))
    rows = lax.broadcasted_iota(jnp.int32, (TOK, PROMPTS), 0)
    doc = doc_of(rows + seq * TOK, ends)
    slots = pick(doc, [slot_ref[window * DOCS + j] for j in range(DOCS)], jnp.int32)
    lanes = lax.broadcasted_iota(jnp.int32, (TOK, PROMPTS), 1)
    chosen = jnp.where(lanes == (slots >> 4), 1.0, 0.0).astype(jnp.bfloat16)
    found = dot(chosen, pieces, NT)
    lanes = lanes[:, :48]
    found = jnp.where((lanes & 15) == (slots[:, :48] & 15), found, 0.0)
    lengths = [len_ref[0, j].astype(jnp.float32) for j in range(DOCS)]
    token_grad = jnp.sum(found, axis=1, keepdims=True) / pick(doc[:, :1], lengths, jnp.float32)
    leaving = []
    for g in range(KVH):
        at = block_of(g)
        keys = jnp.concatenate([kh_ref[:, at], kl_ref[:, at]], axis=0)
        values = jnp.concatenate([vh_ref[:, at], vl_ref[:, at]], axis=0)
        queries = stack_heads(q_ref, g)
        out_grad = jnp.concatenate(
            [(token_grad * u_ref[:, block_of(REP * g + i)]).astype(jnp.bfloat16) for i in range(REP)],
            axis=0,
        )
        soft = p_ref[g]
        prob_grad = dot(out_grad, values, NT)
        wide = soft.astype(jnp.float32)
        delta = jnp.sum(wide * prob_grad, axis=1, keepdims=True)
        score_grad = (wide * ((prob_grad - delta) * HD ** (-0.5))).astype(jnp.bfloat16)
        dk = dot(score_grad, queries, TN).astype(jnp.bfloat16)
        dv = dot(soft, out_grad, TN).astype(jnp.bfloat16)
        back_ref[:, at] = dk[:TOK]
        back_ref[:, KVD + g * HD : KVD + (g + 1) * HD] = dv[:TOK]
        dk_ref[:, at] = dk[TOK:]
        dv_ref[:, at] = dv[TOK:]
        dq = dot(score_grad, keys, NN).astype(jnp.bfloat16)
        for i in range(REP):
            qg_ref[:, block_of(REP * g + i)] = dq[i * TOK : (i + 1) * TOK]
        to = slice(g * REP * HD, (g + 1) * REP * HD)
        leaving += start_all([(qg_ref.at[:, to], qg_hbm.at[:, to])], out_sems.at[g : g + 1])
    for copy in leaving:
        copy.wait()


def finish_kernel(r_ref, gain_ref, head_ref, dk_ref, dv_ref, back_ref, kg_ref, vg_ref, gg_ref, hg_ref, flat_ref):
    for a in range(N_RING):
        flat_ref[PER * a : PER * (a + 1), :] = r_ref[a, 0:PER, :]
    total = flat_ref[0 : D // LANES, :]
    gg_ref[...] = head_ref[...] * total
    hg_ref[...] = gain_ref[...] * total
    f32 = jnp.float32
    kg_ref[...] = (dk_ref[...].astype(f32) + back_ref[:, :KVD].astype(f32)).astype(jnp.bfloat16)
    vg_ref[...] = (dv_ref[...].astype(f32) + back_ref[:, KVD:].astype(f32)).astype(jnp.bfloat16)


VM = pl.BlockSpec(memory_space=pltpu.VMEM)
SM = pl.BlockSpec(memory_space=pltpu.SMEM)
ANY = pl.BlockSpec(memory_space=pl.ANY)


def shape(dims, dtype):
    return jax.ShapeDtypeStruct(dims, dtype)


def cost(flops, moved):
    return pl.CostEstimate(flops=flops, bytes_accessed=moved, transcendentals=0)


def along_seq(block, distance):
    count = NH * NC
    route = [(i, i + distance) for i in range(count) if 0 <= i + distance < count]
    return lax.ppermute(block, ("h", "c"), route)


def exchange(block, axes):
    return lax.all_to_all(block, axes, 0, 0, tiled=True)


def per_device(
    query_states, key_states, value_states, residual, norm_gain, reward_head, lengths, response_slot
):
    bf, f32 = jnp.bfloat16, jnp.float32
    far_keys = along_seq(key_states, 1)
    far_values = along_seq(value_states, 1)
    dma = pltpu.SemaphoreType.DMA
    limit = pltpu.CompilerParams(vmem_limit_bytes=24 * 1024 * 1024)
    queries, keys, values, resid, weights = pl.pallas_call(
        local_kernel,
        in_specs=[SM] + [ANY] * 4,
        out_specs=[VM] * 5,
        out_shape=[
            shape((TOK, D), bf), shape((TOK, KVD), bf), shape((TOK, KVD), bf), shape((TOK, D), bf),
            shape((KVH, REP * TOK, TOK), f32),
        ],
        scratch_shapes=[dma((4,))],
        compiler_params=limit,
        cost_estimate=cost(140000000, 8000000),
        name="local",
    )(lengths, query_states, key_states, value_states, residual)
    soft, unscaled, sums = pl.pallas_call(
        forward_kernel,
        in_specs=[SM] * 2 + [VM] * 8,
        out_specs=[VM] * 3,
        out_shape=[
            shape((KVH, REP * TOK, 2 * TOK), bf),
            shape((TOK, D), f32),
            shape((N_RING, DOCS, WIDE + LANES), f32),
        ],
        scratch_shapes=[pltpu.VMEM((TOK, D), f32)],
        compiler_params=limit,
        cost_estimate=cost(400000000, 8000000),
        name="forward",
    )(
        lengths, response_slot, queries, far_keys, far_values, values, resid, weights,
        norm_gain.reshape(1, D), reward_head.reshape(1, D),
    )
    sums = exchange(sums, RING)
    sums = pl.pallas_call(
        turn_kernel,
        in_specs=[VM],
        out_specs=VM,
        out_shape=shape((N_PLANE, PER + 1, LANES), f32),
        scratch_shapes=[pltpu.VMEM((WIDE // 2, LANES), f32)],
        compiler_params=pltpu.CompilerParams(vmem_limit_bytes=8 * 1024 * 1024),
        name="turn",
    )(sums)
    sums = exchange(sums, PLANE)
    query_grad, back, key_part, value_part, total, loss = pl.pallas_call(
        backward_kernel,
        in_specs=[SM] * 2 + [VM] * 8,
        out_specs=[ANY] + [VM] * 4 + [SM],
        out_shape=[
            shape((TOK, D), bf),
            shape((TOK, 2 * KVD), bf),
            shape((TOK, KVD), bf),
            shape((TOK, KVD), bf),
            shape((N_PLANE, PER + 1, LANES), f32),
            shape((1, 1), f32),
        ],
        scratch_shapes=[
            pltpu.VMEM((TOK, D), bf), pltpu.VMEM((COLUMNS, PER + 1, LANES), f32), dma((8,)),
        ],
        compiler_params=limit,
        cost_estimate=cost(1080000000, 9000000),
        name="backward",
    )(
        lengths, response_slot, sums, queries, far_keys, far_values, keys, values, soft, unscaled
    )
    returned = along_seq(back, -1)
    total = exchange(total, PLANE)
    total = jnp.broadcast_to(jnp.sum(total, axis=0, keepdims=True), (N_RING, PER + 1, LANES))
    total = exchange(total, RING)
    square = (D // LANES, LANES)
    key_grad, value_grad, gain_grad, head_grad = pl.pallas_call(
        finish_kernel,
        in_specs=[VM] * 6,
        out_specs=[VM] * 4,
        out_shape=[
            shape((TOK, KVD), bf), shape((TOK, KVD), bf), shape(square, f32), shape(square, f32),
        ],
        scratch_shapes=[pltpu.VMEM((40, LANES), f32)],
        compiler_params=pltpu.CompilerParams(vmem_limit_bytes=16 * 1024 * 1024),
        name="finish",
    )(total, norm_gain.reshape(square), reward_head.reshape(square), key_part, value_part, returned)
    return (
        loss.reshape(()), query_grad, key_grad, value_grad, gain_grad.reshape(D), head_grad.reshape(D)
    )


def solution(mesh):
    axes = ("y", "l", "x", "h", "c")
    inner = Mesh(mesh.devices.reshape(NY, NL, NX, NH, NC), axes)
    dp, rows = ("y", "l", "x"), P(axes, None)
    return jax.shard_map(
        per_device,
        mesh=inner,
        in_specs=(rows, rows, rows, rows, P(), P(), P(dp, None), P()),
        out_specs=(P(), rows, rows, rows, P(), P()),
        check_vma=False,
    )
```

time: 149 us -> 125 us (0.84)
  blocking collectives: 59.9 us -> 84.5 us
  starting transfers between devices: 44.9 us -> 20.5 us
  local copies, waits for them, and re-layouts: 23.4 us -> 5.01 us
  waiting for transfers between devices: 5.55 us -> 0.01 us
  Pallas kernels: 10.8 us -> 13.6 us
  other arithmetic: 2.75 us -> 0.08 us
    all_to_all x3 -> x4, blocking collectives: 59.9 us -> 84.5 us  [exchange(): return lax.all_to_all(block, axes, 0, 0, tiled=True)]
    all_to_all x1 -> x0, starting transfers between devices: 21.8 us -> none  [exchange(): return lax.all_to_all(block, axes, 0, 0, tiled=True)]
    unnamed x46 -> x16, local copies, waits for them, and re-layouts: 15.1 us -> 5.01 us
    reshape x5 -> x0, local copies, waits for them, and re-layouts: 6.79 us -> none  [the longest x3 4.36 us: per_device(): response_slot.reshape(NY, NL, NX, 2, 4).transpose(3, 1, 4, 0, 2)]
    ppermute x3, waiting for transfers between devices: 4.49 us -> 0.01 us  [along_seq(): return lax.ppermute(block, ('h', 'c'), route)]
    pallas_call x2 -> x4, Pallas kernels: 10 us -> 13.5 us  [the longest x1 7.72 us: per_device(): pl.pallas_call(backward_kernel, in_specs=[SM] * 2 + [VM] * 8, out_specs=[...]
    ppermute x3, starting transfers between devices: 23 us -> 20.5 us  [along_seq(): return lax.ppermute(block, ('h', 'c'), route)]
    convert_element_type x2 -> x0, other arithmetic: 2.06 us -> none  [the longest x1 1.97 us: per_device(): value_grad = (value_part.astype(f32) + returned[:, KVD:]).astype(bf)]
  transfers between devices with their start and end apart: 4 -> 3, of which waited for: 3 -> 0; matrix products, arithmetic and copies ran while one was open for 6% -> 0% of each run, Pallas kernels for 0% -> 1%
where the time goes in v2:
time: 125 us; the launch traced here: 124 us
  blocking collectives  84.5 us (68%)
  starting transfers between devices  20.5 us (16%)
  Pallas kernels  13.6 us (11%)
  local copies, waits for them, and re-layouts  5.01 us (4%)
    all_to_all x4, blocking collectives, exchange(): return lax.all_to_all(block, axes, 0, 0, tiled=True)  84.5 us
    ppermute x3, starting transfers between devices, along_seq(): return lax.ppermute(block, ('h', 'c'), route)  20.5 us
    pallas_call x1, Pallas kernels, per_device(): pl.pallas_call(backward_kernel, in_specs=[SM] * 2 + [VM] * 8, out_specs=[...  7.72 us
    unnamed x16, local copies, waits for them, and re-layouts  5.01 us
    pallas_call x1, Pallas kernels, per_device(): pl.pallas_call(forward_kernel, in_specs=[SM] * 2 + [VM] * 8, out_specs=[V...  3.53 us
  transfers between devices with their start and end apart: 3, of which 0 were waited for; matrix products, arithmetic and copies ran while one was open for 0% of the time, Pallas kernels for 1%

profile of v2, /device:TPU:1, one launch (start us, length us, event | category | flops | bytes accessed | tf_op | source)
XLA Modules:
  0.0 124.5 jit_solution(5034499300366437887)
XLA Ops:
  0.6 16.2 %collective-permute-start = (bf16[128,1024]{1,0:T(8,128)(2,1)}, bf16[128,1024]{1,0:T(8,128)(2,1)S(1)}, u32[]{:S(2)}, u32[]{:S(2)}) collective-permute-start(bf16[128,1024]{1,0:T(8,128)(2,1)} %kl_hbm.1), channel_id=1, source_target_pairs={{0,1},{1,2},{2,3},{4,5},{5,6},{6,7},{8,9},{9,10},{10,11},{12,13},{... | collective-permute-start | bytes 786440 | tf_op jit(solution)/shard_map/ppermute | solution.py:324
  16.9 1.9 %collective-permute-start.1 = (bf16[128,1024]{1,0:T(8,128)(2,1)}, bf16[128,1024]{1,0:T(8,128)(2,1)S(1)}, u32[]{:S(2)}, u32[]{:S(2)}) collective-permute-start(bf16[128,1024]{1,0:T(8,128)(2,1)} %vl_hbm.1), channel_id=1, source_target_pairs={{0,1},{1,2},{2,3},{4,5},{5,6},{6,7},{8,9},{9,10},{10,11},{12,13},{... | collective-permute-start | bytes 786440 | tf_op jit(solution)/shard_map/ppermute | solution.py:324
  18.8 0.0 copy-start
  18.8 1.2 copy-done
  20.0 0.0 copy-start.1
  20.0 1.2 copy-done.1
  21.3 0.0 copy-start.2
  21.3 0.9 copy-done.2
  22.2 0.0 copy-start.3
  22.2 0.9 copy-done.3
  23.2 0.0 copy-start.7
  23.2 0.7 copy-done.7
  23.8 0.0 copy-start.4
  23.8 0.0 copy-start.5
  23.8 0.0 copy-start.6
  23.8 1.3 %local.1 = (bf16[128,4096]{1,0:T(8,128)(2,1)S(1)}, bf16[128,1024]{1,0:T(8,128)(2,1)S(1)}, bf16[128,1024]{1,0:T(8,128)(2,1)S(1)}, bf16[128,4096]{1,0:T(8,128)(2,1)S(1)}, f32[8,512,128]{2,1,0:T(8,128)S(1)}) custom-call(s32[1,8]{1,0:T(1,128)S(1)} %copy-done.7, bf16[128,4096]{1,0:T(8,128)(2,1)S(1)} %copy-done, bf16[128,1024]{1,0:T(8,128)(2,1)S(1)} %copy-done.2, ...), custom_call_target="tpu_custom_call" | custom-call | flops 140000000 | bytes 8000000 | tf_op jit(solution)/shard_map/local/pallas_call | solution.py:339
  25.1 0.0 collective-permute-done.kh_ref
  25.1 0.0 collective-permute-done.1.vh_ref
  25.1 0.0 copy-done.4
  25.2 0.0 copy-done.5
  25.2 0.0 copy-done.6
  25.2 3.5 %forward.1 = (bf16[8,512,256]{2,1,0:T(8,128)(2,1)S(1)}, f32[128,4096]{1,0:T(8,128)S(1)}, f32[12,8,512]{2,1,0:T(8,128)S(1)}) custom-call(s32[1,8]{1,0:T(1,128)S(1)} %copy-done.7, s32[1536]{0:T(1024)S(1)} %copy-done.6, bf16[128,4096]{1,0:T(8,128)(2,1)S(1)} %get-tuple-element.24.q_ref, bf16[128,1024]{1,0:T(8,128)(2,1)S(1)} %collective-permute-done.kh_ref, ...), custom_call_target="tpu_custom_call" | custom-call | flops 400000000 | bytes 8000000 | tf_op jit(solution)/shard_map/forward/pallas_call | solution.py:352
  28.7 24.9 %all_to_all.20.r_ref = f32[12,8,512]{2,1,0:T(8,128)S(1)} all-to-all(f32[12,8,512]{2,1,0:T(8,128)S(1)} %get-tuple-element.28), channel_id=1, replica_groups=mesh['y'=8,'l'=6,'x'=4,'h'=2,'c'=2] {'l','h'}, dimensions={0} | all-to-all | bytes 393216 | tf_op jit(solution)/shard_map/all_to_all | solution.py:328
  53.6 0.2 turn.1
  53.8 27.2 %all_to_all.21.r_ref = f32[64,4,128]{2,1,0:T(4,128)S(1)} all-to-all(f32[64,4,128]{2,1,0:T(4,128)S(1)} %turn.1), channel_id=1, replica_groups=mesh['y'=8,'l'=6,'x'=4,'h'=2,'c'=2] {'y','x','c'}, dimensions={0} | all-to-all | bytes 262144 | tf_op jit(solution)/shard_map/all_to_all | solution.py:328
  81.0 7.7 %backward.1 = (bf16[128,4096]{1,0:T(8,128)(2,1)}, bf16[128,2048]{1,0:T(8,128)(2,1)S(1)}, bf16[128,1024]{1,0:T(8,128)(2,1)S(1)}, bf16[128,1024]{1,0:T(8,128)(2,1)...) custom-call(s32[1,8]{1,0:T(1,128)S(1)} %copy-done.7, s32[1536]{0:T(1024)S(1)} %copy-done.6, ...), custom_call_target="tpu_custom_call" | custom-call | flops 1080000000 | bytes 9000000 | tf_op jit(solution)/shard_map/backward/pallas_call | solution.py:380
  88.7 2.3 %collective-permute-start.2 = (bf16[128,2048]{1,0:T(8,128)(2,1)S(1)}, bf16[128,2048]{1,0:T(8,128)(2,1)S(1)}, u32[]{:S(2)}, u32[]{:S(2)}) collective-permute-start(bf16[128,2048]{1,0:T(8,128)(2,1)S(1)} %get-tuple-element.37), channel_id=1, source_target_pairs={{1,0},{2,1},{3,2},{5,4},{6,5},{7,6},{9,8},{10,9},{11,10},{13,12},{... | collective-permute-start | bytes 1572872 | tf_op jit(solution)/shard_map/ppermute | solution.py:324
  91.0 14.6 %all_to_all.22 = f32[64,4,128]{2,1,0:T(4,128)S(1)} all-to-all(f32[64,4,128]{2,1,0:T(4,128)S(1)} %get-tuple-element.34), channel_id=1, replica_groups=mesh['y'=8,'l'=6,'x'=4,'h'=2,'c'=2] {'y','x','c'}, dimensions={0} | all-to-all | bytes 262144 | tf_op jit(solution)/shard_map/all_to_all | solution.py:328
  105.7 0.1 reduce_sum.9
  105.8 17.7 %all_to_all.23.r_ref = f32[12,4,128]{2,1,0:T(4,128)S(1)} all-to-all(f32[12,4,128]{2,1,0:T(4,128)S(1)} %broadcast_in_dim.2), channel_id=1, replica_groups=mesh['y'=8,'l'=6,'x'=4,'h'=2,'c'=2] {'l','h'}, dimensions={0} | all-to-all | bytes 49152 | tf_op jit(solution)/shard_map/all_to_all | solution.py:328
  123.5 0.0 collective-permute-done.2.back_ref
  123.5 0.9 finish.1
  (1 shorter events, 0.0 us)
Async XLA Ops:
  0.6 24.5 %collective-permute-start = (bf16[128,1024]{1,0:T(8,128)(2,1)}, bf16[128,1024]{1,0:T(8,128)(2,1)S(1)}, u32[]{:S(2)}, u32[]{:S(2)}) collective-permute-start(bf16[128,1024]{1,0:T(8,128)(2,1)} %kl_hbm.1), channel_id=1, source_target_pairs={{0,1},{1,2},{2,3},{4,5},{5,6},{6,7},{8,9},{9,10},{10,11},{12,13},{... | collective-permute-start | bytes 786440 | tf_op jit(solution)/shard_map/ppermute | solution.py:324
  16.9 8.2 %collective-permute-start.1 = (bf16[128,1024]{1,0:T(8,128)(2,1)}, bf16[128,1024]{1,0:T(8,128)(2,1)S(1)}, u32[]{:S(2)}, u32[]{:S(2)}) collective-permute-start(bf16[128,1024]{1,0:T(8,128)(2,1)} %vl_hbm.1), channel_id=1, source_target_pairs={{0,1},{1,2},{2,3},{4,5},{5,6},{6,7},{8,9},{9,10},{10,11},{12,13},{... | collective-permute-start | bytes 786440 | tf_op jit(solution)/shard_map/ppermute | solution.py:324
  18.8 1.2 copy-start
  20.0 1.2 copy-start.1
  21.3 0.9 copy-start.2
  22.2 0.9 copy-start.3
  23.2 0.7 copy-start.7
  23.8 1.3 %copy-start.4 = (f32[4096]{0:T(1024)S(1)}, f32[4096]{0:T(1024)}, u32[]{:S(2)}) copy-start(f32[4096]{0:T(1024)} %param.12) | copy-start | bytes 49156
  23.8 1.3 %copy-start.5 = (f32[4096]{0:T(1024)S(1)}, f32[4096]{0:T(1024)}, u32[]{:S(2)}) copy-start(f32[4096]{0:T(1024)} %param.13) | copy-start | bytes 49156
  23.8 1.3 %copy-start.6 = (s32[1536]{0:T(1024)S(1)}, s32[1536]{0:T(1024)}, u32[]{:S(2)}) copy-start(s32[1536]{0:T(1024)} %slot_ref.3) | copy-start | bytes 18436
  88.7 34.8 %collective-permute-start.2 = (bf16[128,2048]{1,0:T(8,128)(2,1)S(1)}, bf16[128,2048]{1,0:T(8,128)(2,1)S(1)}, u32[]{:S(2)}, u32[]{:S(2)}) collective-permute-start(bf16[128,2048]{1,0:T(8,128)(2,1)S(1)} %get-tuple-element.37), channel_id=1, source_target_pairs={{1,0},{2,1},{3,2},{5,4},{6,5},{7,6},{9,8},{10,9},{11,10},{13,12},{... | collective-permute-start | bytes 1572872 | tf_op jit(solution)/shard_map/ppermute | solution.py:324

commit v3 on v2

--- a/solution.py
+++ b/solution.py
@@ -90,7 +90,7 @@
 
 
 def weigh(queries, keys, mask):
-    scores = dot(queries, keys, NT)
+    scores = dot(keys, queries, NT)
     return jnp.exp2(scores * (HD ** (-0.5) * LOG2E)) * mask
 
 
@@ -104,8 +104,8 @@
     cols = lax.broadcasted_iota(jnp.int32, (TOK, TOK), 1)
     base = seq * TOK
     same = doc_of(rows + base, ends) == doc_of(cols + base, ends)
-    mask = jnp.where(same & (cols <= rows), 1.0, 0.0)
-    mask = jnp.concatenate([mask] * REP, axis=0)
+    mask = jnp.where(same & (rows <= cols), 1.0, 0.0)
+    mask = jnp.concatenate([mask] * REP, axis=1)
     copies[0].wait()
     copies[1].wait()
     for g in range(KVH):
@@ -124,21 +124,21 @@
     cols = lax.broadcasted_iota(jnp.int32, (TOK, TOK), 1)
     base = seq * TOK
     doc_r = doc_of(rows + base, ends)
-    doc_h = jnp.where(seq > 0, doc_of(cols + base - TOK, ends), -1)
-    mask = jnp.where(doc_r == doc_h, 1.0, 0.0)
-    mask = jnp.concatenate([mask] * REP, axis=0)
+    doc_h = jnp.where(seq > 0, doc_of(rows + base - TOK, ends), -1)
+    mask = jnp.where(doc_h == doc_of(cols + base, ends), 1.0, 0.0)
+    mask = jnp.concatenate([mask] * REP, axis=1)
     squares = jnp.zeros((TOK, HD), jnp.float32)
     scored = jnp.zeros((TOK, HD), jnp.float32)
     for g in range(KVH):
         at = block_of(g)
         values = jnp.concatenate([vh_ref[:, at], vl_ref[:, at]], axis=0)
         weights = jnp.concatenate(
-            [weigh(stack_heads(q_ref, g), kh_ref[:, at], mask), w_ref[g]], axis=1
+            [weigh(stack_heads(q_ref, g), kh_ref[:, at], mask), w_ref[g]], axis=0
         )
-        totals = jnp.sum(weights, axis=1, keepdims=True)
+        totals = jnp.sum(weights, axis=0, keepdims=True)
         soft = (weights * (1.0 / totals)).astype(jnp.bfloat16)
         p_ref[g] = soft
-        out = dot(soft, values, NN)
+        out = dot(soft, values, TN)
         for i in range(REP):
             to = block_of(REP * g + i)
             hidden = res_ref[:, to].astype(jnp.float32) + out[i * TOK : (i + 1) * TOK]
@@ -191,9 +191,9 @@
     second = jnp.concatenate([empty, docs], axis=0).T
     flat_ref[...] = first[: WIDE // 2] + second[WIDE // 2 : WIDE]
     extra = first[WIDE : WIDE + 1] + second[WIDE + 64 : WIDE + 65]
-    for b in range(N_PLANE):
-        x_ref[b, 0:PER, :] = flat_ref[b * PER : (b + 1) * PER, :]
-        x_ref[b, PER : PER + 1, :] = extra
+    for i in range(PER):
+        x_ref[:, i, :] = flat_ref[i * N_PLANE : (i + 1) * N_PLANE, :]
+    x_ref[:, PER, :] = jnp.broadcast_to(extra, (N_PLANE, LANES))
 
 
 def backward_kernel(
@@ -201,9 +201,7 @@
     qg_hbm, back_ref, dk_ref, dv_ref, x_ref, loss_ref,
     qg_ref, sum_ref, out_sems,
 ):
-    core = lax.axis_index("c")
     seq, window = window_place()
-    plane_at = (lax.axis_index("y") * NX + lax.axis_index("x")) * NC + core
     ends = ends_of(len_ref)
     got = r_ref[...].reshape(COLUMNS, NC, PER + 1, LANES)
     sum_ref[...] = got[:, 0] + got[:, 1]
@@ -247,13 +245,9 @@
     lane = lax.broadcasted_iota(jnp.int32, (PER + 1, LANES), 1)
     first = jnp.sum(jnp.where(lane < 64, total, 0.0), axis=1, keepdims=True)
     second = jnp.sum(jnp.where(lane < 64, 0.0, total), axis=1, keepdims=True)
-    feature = row * LANES + lane
-    placed = jnp.zeros((PER + 1, LANES), jnp.float32)
-    for i in range(PER):
-        to = plane_at * PER + i
-        placed = jnp.where(feature == to, first[i : i + 1], placed)
-        placed = jnp.where(feature == to + WIDE // 2, second[i : i + 1], placed)
-    x_ref[...] = jnp.broadcast_to(placed[None], (N_PLANE, PER + 1, LANES))
+    placed = jnp.where(row == lane, first, 0.0) + jnp.where(row + PER == lane, second, 0.0)
+    placed = jnp.sum(jnp.where(row < PER, placed, 0.0), axis=0, keepdims=True)
+    x_ref[...] = jnp.broadcast_to(placed, (N_PLANE, LANES))
     rows = lax.broadcasted_iota(jnp.int32, (TOK, PROMPTS), 0)
     doc = doc_of(rows + seq * TOK, ends)
     slots = pick(doc, [slot_ref[window * DOCS + j] for j in range(DOCS)], jnp.int32)
@@ -275,17 +269,17 @@
             axis=0,
         )
         soft = p_ref[g]
-        prob_grad = dot(out_grad, values, NT)
+        prob_grad = dot(values, out_grad, NT)
         wide = soft.astype(jnp.float32)
-        delta = jnp.sum(wide * prob_grad, axis=1, keepdims=True)
+        delta = jnp.sum(wide * prob_grad, axis=0, keepdims=True)
         score_grad = (wide * ((prob_grad - delta) * HD ** (-0.5))).astype(jnp.bfloat16)
-        dk = dot(score_grad, queries, TN).astype(jnp.bfloat16)
-        dv = dot(soft, out_grad, TN).astype(jnp.bfloat16)
+        dk = dot(score_grad, queries, NN).astype(jnp.bfloat16)
+        dv = dot(soft, out_grad, NN).astype(jnp.bfloat16)
         back_ref[:, at] = dk[:TOK]
         back_ref[:, KVD + g * HD : KVD + (g + 1) * HD] = dv[:TOK]
         dk_ref[:, at] = dk[TOK:]
         dv_ref[:, at] = dv[TOK:]
-        dq = dot(score_grad, keys, NN).astype(jnp.bfloat16)
+        dq = dot(score_grad, keys, TN).astype(jnp.bfloat16)
         for i in range(REP):
             qg_ref[:, block_of(REP * g + i)] = dq[i * TOK : (i + 1) * TOK]
         to = slice(g * REP * HD, (g + 1) * REP * HD)
@@ -294,15 +288,31 @@
         copy.wait()
 
 
-def finish_kernel(r_ref, gain_ref, head_ref, dk_ref, dv_ref, back_ref, kg_ref, vg_ref, gg_ref, hg_ref, flat_ref):
+def pass_kernel(r_ref, x_ref):
+    got = r_ref[...]
+    empty = jnp.zeros_like(got)
+    even = jnp.concatenate([got, empty], axis=0).T
+    odd = jnp.concatenate([empty, got], axis=0).T
+    for i in range(PER):
+        line = even[2 * i : 2 * i + 1] + odd[2 * i + 1 : 2 * i + 2]
+        x_ref[:, i, :] = jnp.broadcast_to(line, (N_RING, LANES))
+    x_ref[:, PER, :] = jnp.zeros((N_RING, LANES), jnp.float32)
+
+
+def finish_kernel(
+    r_ref, gain_ref, head_ref, dk_ref, dv_ref, across_ref, beside_ref,
+    kg_ref, vg_ref, gg_ref, hg_ref, flat_ref,
+):
     for a in range(N_RING):
         flat_ref[PER * a : PER * (a + 1), :] = r_ref[a, 0:PER, :]
     total = flat_ref[0 : D // LANES, :]
     gg_ref[...] = head_ref[...] * total
     hg_ref[...] = gain_ref[...] * total
     f32 = jnp.float32
-    kg_ref[...] = (dk_ref[...].astype(f32) + back_ref[:, :KVD].astype(f32)).astype(jnp.bfloat16)
-    vg_ref[...] = (dv_ref[...].astype(f32) + back_ref[:, KVD:].astype(f32)).astype(jnp.bfloat16)
+    seq, _ = window_place()
+    returned = jnp.where(seq == 1, across_ref[...], beside_ref[...]).astype(f32)
+    kg_ref[...] = (dk_ref[...].astype(f32) + returned[:, :KVD]).astype(jnp.bfloat16)
+    vg_ref[...] = (dv_ref[...].astype(f32) + returned[:, KVD:]).astype(jnp.bfloat16)
 
 
 VM = pl.BlockSpec(memory_space=pltpu.VMEM)
@@ -318,9 +328,7 @@
     return pl.CostEstimate(flops=flops, bytes_accessed=moved, transcendentals=0)
 
 
-def along_seq(block, distance):
-    count = NH * NC
-    route = [(i, i + distance) for i in range(count) if 0 <= i + distance < count]
+def along_seq(block, route):
     return lax.ppermute(block, ("h", "c"), route)
 
 
@@ -332,8 +340,8 @@
     query_states, key_states, value_states, residual, norm_gain, reward_head, lengths, response_slot
 ):
     bf, f32 = jnp.bfloat16, jnp.float32
-    far_keys = along_seq(key_states, 1)
-    far_values = along_seq(value_states, 1)
+    far_keys = along_seq(key_states, [(0, 1), (1, 2), (2, 3)])
+    far_values = along_seq(value_states, [(0, 1), (1, 2), (2, 3)])
     dma = pltpu.SemaphoreType.DMA
     limit = pltpu.CompilerParams(vmem_limit_bytes=24 * 1024 * 1024)
     queries, keys, values, resid, weights = pl.pallas_call(
@@ -342,7 +350,7 @@
         out_specs=[VM] * 5,
         out_shape=[
             shape((TOK, D), bf), shape((TOK, KVD), bf), shape((TOK, KVD), bf), shape((TOK, D), bf),
-            shape((KVH, REP * TOK, TOK), f32),
+            shape((KVH, TOK, REP * TOK), f32),
         ],
         scratch_shapes=[dma((4,))],
         compiler_params=limit,
@@ -354,7 +362,7 @@
         in_specs=[SM] * 2 + [VM] * 8,
         out_specs=[VM] * 3,
         out_shape=[
-            shape((KVH, REP * TOK, 2 * TOK), bf),
+            shape((KVH, 2 * TOK, REP * TOK), bf),
             shape((TOK, D), f32),
             shape((N_RING, DOCS, WIDE + LANES), f32),
         ],
@@ -386,7 +394,7 @@
             shape((TOK, 2 * KVD), bf),
             shape((TOK, KVD), bf),
             shape((TOK, KVD), bf),
-            shape((N_PLANE, PER + 1, LANES), f32),
+            shape((N_PLANE, LANES), f32),
             shape((1, 1), f32),
         ],
         scratch_shapes=[
@@ -398,14 +406,23 @@
     )(
         lengths, response_slot, sums, queries, far_keys, far_values, keys, values, soft, unscaled
     )
-    returned = along_seq(back, -1)
+    across = along_seq(back, [(2, 1)])
     total = exchange(total, PLANE)
-    total = jnp.broadcast_to(jnp.sum(total, axis=0, keepdims=True), (N_RING, PER + 1, LANES))
+    total = pl.pallas_call(
+        pass_kernel,
+        in_specs=[VM],
+        out_specs=VM,
+        out_shape=shape((N_RING, PER + 1, LANES), f32),
+        compiler_params=pltpu.CompilerParams(vmem_limit_bytes=8 * 1024 * 1024),
+        name="pass",
+    )(total)
+    total, back = lax.optimization_barrier((total, back))
+    beside = along_seq(back, [(1, 0), (3, 2)])
     total = exchange(total, RING)
     square = (D // LANES, LANES)
     key_grad, value_grad, gain_grad, head_grad = pl.pallas_call(
         finish_kernel,
-        in_specs=[VM] * 6,
+        in_specs=[VM] * 7,
         out_specs=[VM] * 4,
         out_shape=[
             shape((TOK, KVD), bf), shape((TOK, KVD), bf), shape(square, f32), shape(square, f32),
@@ -413,7 +430,7 @@
         scratch_shapes=[pltpu.VMEM((40, LANES), f32)],
         compiler_params=pltpu.CompilerParams(vmem_limit_bytes=16 * 1024 * 1024),
         name="finish",
-    )(total, norm_gain.reshape(square), reward_head.reshape(square), key_part, value_part, returned)
+    )(total, norm_gain.reshape(square), reward_head.reshape(square), key_part, value_part, across, beside)
     return (
         loss.reshape(()), query_grad, key_grad, value_grad, gain_grad.reshape(D), head_grad.reshape(D)
     )

time: 125 us -> 121 us (0.968)
  blocking collectives: 84.5 us -> 66.3 us
  waiting for transfers between devices: 0.01 us -> 8.12 us
  starting transfers between devices: 20.5 us -> 26.5 us
    all_to_all x4 -> x3, blocking collectives: 84.5 us -> 66.3 us  [exchange(): return lax.all_to_all(block, axes, 0, 0, tiled=True)]
    all_to_all x0 -> x1, waiting for transfers between devices: none -> 8.11 us  [exchange(): return lax.all_to_all(block, axes, 0, 0, tiled=True)]
    all_to_all x0 -> x1, starting transfers between devices: none -> 4.43 us  [exchange(): return lax.all_to_all(block, axes, 0, 0, tiled=True)]
    ppermute x3 -> x4, starting transfers between devices: 20.5 us -> 22.1 us  [along_seq(): return lax.ppermute(block, ('h', 'c'), route)]
  transfers between devices with their start and end apart: 3 -> 5, of which waited for: 0 -> 1; matrix products, arithmetic and copies ran while one was open for 0% -> 0% of each run, Pallas kernels for 1% -> 1%
where the time goes in v3:
time: 121 us; the launch traced here: 120 us
  blocking collectives  66.3 us (55%)
  starting transfers between devices  26.5 us (22%)
  Pallas kernels  13.4 us (11%)
  waiting for transfers between devices  8.12 us (7%)
  local copies, waits for them, and re-layouts  5.01 us (4%)
    all_to_all x3, blocking collectives, exchange(): return lax.all_to_all(block, axes, 0, 0, tiled=True)  66.3 us
    ppermute x4, starting transfers between devices, along_seq(): return lax.ppermute(block, ('h', 'c'), route)  22.1 us
    all_to_all x1, waiting for transfers between devices, exchange(): return lax.all_to_all(block, axes, 0, 0, tiled=True)  8.11 us
    pallas_call x1, Pallas kernels, per_device(): pl.pallas_call(backward_kernel, in_specs=[SM] * 2 + [VM] * 8, out_specs=[...  7.19 us
    unnamed x16, local copies, waits for them, and re-layouts  5.01 us
    all_to_all x1, starting transfers between devices, exchange(): return lax.all_to_all(block, axes, 0, 0, tiled=True)  4.43 us
    pallas_call x1, Pallas kernels, per_device(): pl.pallas_call(forward_kernel, in_specs=[SM] * 2 + [VM] * 8, out_specs=[V...  3.66 us
  transfers between devices with their start and end apart: 5, of which 1 were waited for; matrix products, arithmetic and copies ran while one was open for 0% of the time, Pallas kernels for 1%

profile of v3, /device:TPU:1, one launch (start us, length us, event | category | flops | bytes accessed | tf_op | source)
XLA Modules:
  0.0 120.1 jit_solution(6263650508275026510)
XLA Ops:
  0.6 16.2 %collective-permute-start = (bf16[128,1024]{1,0:T(8,128)(2,1)}, bf16[128,1024]{1,0:T(8,128)(2,1)S(1)}, u32[]{:S(2)}, u32[]{:S(2)}) collective-permute-start(bf16[128,1024]{1,0:T(8,128)(2,1)} %kl_hbm.1), channel_id=1, source_target_pairs={{0,1},{1,2},{2,3},{4,5},{5,6},{6,7},{8,9},{9,10},{10,11},{12,13},{... | collective-permute-start | bytes 786440 | tf_op jit(solution)/shard_map/ppermute | solution.py:332
  16.9 1.9 %collective-permute-start.1 = (bf16[128,1024]{1,0:T(8,128)(2,1)}, bf16[128,1024]{1,0:T(8,128)(2,1)S(1)}, u32[]{:S(2)}, u32[]{:S(2)}) collective-permute-start(bf16[128,1024]{1,0:T(8,128)(2,1)} %vl_hbm.1), channel_id=1, source_target_pairs={{0,1},{1,2},{2,3},{4,5},{5,6},{6,7},{8,9},{9,10},{10,11},{12,13},{... | collective-permute-start | bytes 786440 | tf_op jit(solution)/shard_map/ppermute | solution.py:332
  18.8 0.0 copy-start
  18.8 1.2 %copy-done = bf16[128,4096]{1,0:T(8,128)(2,1)S(1)} copy-done((bf16[128,4096]{1,0:T(8,128)(2,1)S(1)}, bf16[128,4096]{1,0:T(8,128)(2,1)}, u32[]{:S(2)}) %copy-start) | copy-done | bytes 1048600
  20.0 0.0 copy-start.1
  20.0 1.2 %copy-done.1 = bf16[128,4096]{1,0:T(8,128)(2,1)S(1)} copy-done((bf16[128,4096]{1,0:T(8,128)(2,1)S(1)}, bf16[128,4096]{1,0:T(8,128)(2,1)}, u32[]{:S(2)}) %copy-start.1) | copy-done | bytes 1048600
  21.3 0.0 copy-start.2
  21.3 0.9 copy-done.2
  22.2 0.0 copy-start.3
  22.2 0.9 copy-done.3
  23.2 0.0 copy-start.7
  23.2 0.7 copy-done.7
  23.8 0.0 copy-start.4
  23.8 0.0 copy-start.5
  23.8 0.0 copy-start.6
  23.8 1.3 %local.1 = (bf16[128,4096]{1,0:T(8,128)(2,1)S(1)}, bf16[128,1024]{1,0:T(8,128)(2,1)S(1)}, bf16[128,1024]{1,0:T(8,128)(2,1)S(1)}, bf16[128,4096]{1,0:T(8,128)(2,1)S(1)}, f32[8,128,512]{2,1,0:T(8,128)S(1)}) custom-call(s32[1,8]{1,0:T(1,128)S(1)} %copy-done.7, bf16[128,4096]{1,0:T(8,128)(2,1)S(1)} %copy-done, bf16[128,1024]{1,0:T(8,128)(2,1)S(1)} %copy-done.2, ...), custom_call_target="tpu_custom_call" | custom-call | flops 140000000 | bytes 8000000 | tf_op jit(solution)/shard_map/local/pallas_call | solution.py:347
  25.1 0.0 collective-permute-done.kh_ref
  25.1 0.0 collective-permute-done.1.vh_ref
  25.1 0.0 copy-done.4
  25.2 0.0 copy-done.5
  25.2 0.0 copy-done.6
  25.2 3.7 %forward.1 = (bf16[8,256,512]{2,1,0:T(8,128)(2,1)S(1)}, f32[128,4096]{1,0:T(8,128)S(1)}, f32[12,8,512]{2,1,0:T(8,128)S(1)}) custom-call(s32[1,8]{1,0:T(1,128)S(1)} %copy-done.7, s32[1536]{0:T(1024)S(1)} %copy-done.6, bf16[128,4096]{1,0:T(8,128)(2,1)S(1)} %get-tuple-element.26.q_ref, bf16[128,1024]{1,0:T(8,128)(2,1)S(1)} %collective-permute-done.kh_ref, ...), custom_call_target="tpu_custom_call" | custom-call | flops 400000000 | bytes 8000000 | tf_op jit(solution)/shard_map/forward/pallas_call | solution.py:360
  28.8 24.9 %all_to_all.26.r_ref = f32[12,8,512]{2,1,0:T(8,128)S(1)} all-to-all(f32[12,8,512]{2,1,0:T(8,128)S(1)} %get-tuple-element.30), channel_id=1, replica_groups=mesh['y'=8,'l'=6,'x'=4,'h'=2,'c'=2] {'l','h'}, dimensions={0} | all-to-all | bytes 393216 | tf_op jit(solution)/shard_map/all_to_all | solution.py:336
  53.7 0.2 turn.1
  53.9 27.2 %all_to_all.27.r_ref = f32[64,4,128]{2,1,0:T(4,128)S(1)} all-to-all(f32[64,4,128]{2,1,0:T(4,128)S(1)} %turn.1), channel_id=1, replica_groups=mesh['y'=8,'l'=6,'x'=4,'h'=2,'c'=2] {'y','x','c'}, dimensions={0} | all-to-all | bytes 262144 | tf_op jit(solution)/shard_map/all_to_all | solution.py:336
  81.1 7.2 %backward.1 = (bf16[128,4096]{1,0:T(8,128)(2,1)}, bf16[128,2048]{1,0:T(8,128)(2,1)S(1)}, bf16[128,1024]{1,0:T(8,128)(2,1)S(1)}, bf16[128,1024]{1,0:T(8,128)(2,1)...) custom-call(s32[1,8]{1,0:T(1,128)S(1)} %copy-done.7, s32[1536]{0:T(1024)S(1)} %copy-done.6, f32[64,4,128]{2,1,0:T(4,128)S(1)} %all_to_all.27.r_ref, ...), custom_call_target="tpu_custom_call" | custom-call | flops 1080000000 | bytes 9000000 | tf_op jit(solution)/shard_map/backward/pallas_call | solution.py:388
  88.3 4.4 %all-to-all-start.2 = ((f32[64,1,128]{2,1,0:T(1,128)}), f32[64,1,128]{2,1,0:T(1,128)S(1)}, u32[]{:S(2)}, u32[]{:S(2)}) async-start(f32[64,1,128]{2,1,0:T(1,128)} %bitcast.4), calls=%async_computation.2 | async-start | bytes 65536 | tf_op jit(solution)/shard_map/all_to_all | solution.py:336
  92.8 1.3 %collective-permute-start.2 = (bf16[128,2048]{1,0:T(8,128)(2,1)S(1)}, bf16[128,2048]{1,0:T(8,128)(2,1)S(1)}, u32[]{:S(2)}, u32[]{:S(2)}) collective-permute-start(bf16[128,2048]{1,0:T(8,128)(2,1)S(1)} %get-tuple-element.41), channel_id=1, source_target_pairs={{2,1},{6,5},{10,9},{14,13},{18,17},{22,21},{26,25},{30,29},{34,33}... | collective-permute-start | bytes 1572872 | tf_op jit(solution)/shard_map/ppermute | solution.py:332
  94.1 8.1 %all-to-all-done.2 = f32[64,1,128]{2,1,0:T(1,128)S(1)} async-done(((f32[64,1,128]{2,1,0:T(1,128)}), f32[64,1,128]{2,1,0:T(1,128)S(1)}, u32[]{:S(2)}, u32[]{:S(2)}) %all-to-all-start.2) | async-done | bytes 32800 | tf_op jit(solution)/shard_map/all_to_all | solution.py:336
  102.2 0.1 pass.1
  102.3 2.6 %collective-permute-start.3 = (bf16[128,2048]{1,0:T(8,128)(2,1)S(1)}, bf16[128,2048]{1,0:T(8,128)(2,1)S(1)}, u32[]{:S(2)}, u32[]{:S(2)}) collective-permute-start(bf16[128,2048]{1,0:T(8,128)(2,1)S(1)} %get-tuple-element.41), channel_id=1, source_target_pairs={{1,0},{3,2},{5,4},{7,6},{9,8},{11,10},{13,12},{15,14},{17,16},{19,... | collective-permute-start | bytes 1572872 | tf_op jit(solution)/shard_map/ppermute | solution.py:332
  104.9 14.2 %all_to_all.28.r_ref = f32[12,4,128]{2,1,0:T(4,128)S(1)} all-to-all(f32[12,4,128]{2,1,0:T(4,128)S(1)} %pass.1), channel_id=1, replica_groups=mesh['y'=8,'l'=6,'x'=4,'h'=2,'c'=2] {'l','h'}, dimensions={0} | all-to-all | bytes 49152 | tf_op jit(solution)/shard_map/all_to_all | solution.py:336
  119.1 0.0 collective-permute-done.2.across_ref
  119.1 0.0 collective-permute-done.3.beside_ref
  119.1 1.0 finish.1
Async XLA Ops:
  0.6 24.5 %collective-permute-start = (bf16[128,1024]{1,0:T(8,128)(2,1)}, bf16[128,1024]{1,0:T(8,128)(2,1)S(1)}, u32[]{:S(2)}, u32[]{:S(2)}) collective-permute-start(bf16[128,1024]{1,0:T(8,128)(2,1)} %kl_hbm.1), channel_id=1, source_target_pairs={{0,1},{1,2},{2,3},{4,5},{5,6},{6,7},{8,9},{9,10},{10,11},{12,13},{... | collective-permute-start | bytes 786440 | tf_op jit(solution)/shard_map/ppermute | solution.py:332
  16.9 8.2 %collective-permute-start.1 = (bf16[128,1024]{1,0:T(8,128)(2,1)}, bf16[128,1024]{1,0:T(8,128)(2,1)S(1)}, u32[]{:S(2)}, u32[]{:S(2)}) collective-permute-start(bf16[128,1024]{1,0:T(8,128)(2,1)} %vl_hbm.1), channel_id=1, source_target_pairs={{0,1},{1,2},{2,3},{4,5},{5,6},{6,7},{8,9},{9,10},{10,11},{12,13},{... | collective-permute-start | bytes 786440 | tf_op jit(solution)/shard_map/ppermute | solution.py:332
  18.8 1.2 %copy-start = (bf16[128,4096]{1,0:T(8,128)(2,1)S(1)}, bf16[128,4096]{1,0:T(8,128)(2,1)}, u32[]{:S(2)}) copy-start(bf16[128,4096]{1,0:T(8,128)(2,1)} %q_hbm.1) | copy-start | bytes 3145732
  20.0 1.2 %copy-start.1 = (bf16[128,4096]{1,0:T(8,128)(2,1)S(1)}, bf16[128,4096]{1,0:T(8,128)(2,1)}, u32[]{:S(2)}) copy-start(bf16[128,4096]{1,0:T(8,128)(2,1)} %res_hbm.1) | copy-start | bytes 3145732
  21.3 0.9 copy-start.2
  22.2 0.9 copy-start.3
  23.2 0.7 copy-start.7
  23.8 1.3 %copy-start.4 = (f32[4096]{0:T(1024)S(1)}, f32[4096]{0:T(1024)}, u32[]{:S(2)}) copy-start(f32[4096]{0:T(1024)} %param.12) | copy-start | bytes 49156
  23.8 1.3 %copy-start.5 = (f32[4096]{0:T(1024)S(1)}, f32[4096]{0:T(1024)}, u32[]{:S(2)}) copy-start(f32[4096]{0:T(1024)} %param.13) | copy-start | bytes 49156
  23.8 1.3 %copy-start.6 = (s32[1536]{0:T(1024)S(1)}, s32[1536]{0:T(1024)}, u32[]{:S(2)}) copy-start(s32[1536]{0:T(1024)} %slot_ref.3) | copy-start | bytes 18436
  88.3 13.8 %all-to-all-start.2 = ((f32[64,1,128]{2,1,0:T(1,128)}), f32[64,1,128]{2,1,0:T(1,128)S(1)}, u32[]{:S(2)}, u32[]{:S(2)}) async-start(f32[64,1,128]{2,1,0:T(1,128)} %bitcast.4), calls=%async_computation.2 | async-start | bytes 65536 | tf_op jit(solution)/shard_map/all_to_all | solution.py:336
  92.8 26.3 %collective-permute-start.2 = (bf16[128,2048]{1,0:T(8,128)(2,1)S(1)}, bf16[128,2048]{1,0:T(8,128)(2,1)S(1)}, u32[]{:S(2)}, u32[]{:S(2)}) collective-permute-start(bf16[128,2048]{1,0:T(8,128)(2,1)S(1)} %get-tuple-element.41), channel_id=1, source_target_pairs={{2,1},{6,5},{10,9},{14,13},{18,17},{22,21},{26,25},{30,29},{34,33}... | collective-permute-start | bytes 1572872 | tf_op jit(solution)/shard_map/ppermute | solution.py:332
  102.3 16.8 %collective-permute-start.3 = (bf16[128,2048]{1,0:T(8,128)(2,1)S(1)}, bf16[128,2048]{1,0:T(8,128)(2,1)S(1)}, u32[]{:S(2)}, u32[]{:S(2)}) collective-permute-start(bf16[128,2048]{1,0:T(8,128)(2,1)S(1)} %get-tuple-element.41), channel_id=1, source_target_pairs={{1,0},{3,2},{5,4},{7,6},{9,8},{11,10},{13,12},{15,14},{17,16},{19,... | collective-permute-start | bytes 1572872 | tf_op jit(solution)/shard_map/ppermute | solution.py:332

commit v4 on v3

--- a/solution.py
+++ b/solution.py
@@ -129,12 +129,16 @@
     mask = jnp.concatenate([mask] * REP, axis=1)
     squares = jnp.zeros((TOK, HD), jnp.float32)
     scored = jnp.zeros((TOK, HD), jnp.float32)
+    def weights_of(g):
+        return weigh(stack_heads(q_ref, g), kh_ref[:, block_of(g)], mask)
+
+    later = weights_of(0)
     for g in range(KVH):
         at = block_of(g)
         values = jnp.concatenate([vh_ref[:, at], vl_ref[:, at]], axis=0)
-        weights = jnp.concatenate(
-            [weigh(stack_heads(q_ref, g), kh_ref[:, at], mask), w_ref[g]], axis=0
-        )
+        weights = jnp.concatenate([later, w_ref[g]], axis=0)
+        if g + 1 < KVH:
+            later = weights_of(g + 1)
         totals = jnp.sum(weights, axis=0, keepdims=True)
         soft = (weights * (1.0 / totals)).astype(jnp.bfloat16)
         p_ref[g] = soft
@@ -259,17 +263,23 @@
     lengths = [len_ref[0, j].astype(jnp.float32) for j in range(DOCS)]
     token_grad = jnp.sum(found, axis=1, keepdims=True) / pick(doc[:, :1], lengths, jnp.float32)
     leaving = []
-    for g in range(KVH):
-        at = block_of(g)
-        keys = jnp.concatenate([kh_ref[:, at], kl_ref[:, at]], axis=0)
-        values = jnp.concatenate([vh_ref[:, at], vl_ref[:, at]], axis=0)
-        queries = stack_heads(q_ref, g)
+    def grads_of(g):
         out_grad = jnp.concatenate(
             [(token_grad * u_ref[:, block_of(REP * g + i)]).astype(jnp.bfloat16) for i in range(REP)],
             axis=0,
         )
+        values = jnp.concatenate([vh_ref[:, block_of(g)], vl_ref[:, block_of(g)]], axis=0)
+        return out_grad, dot(values, out_grad, NT)
+
+    later = grads_of(0)
+    for g in range(KVH):
+        at = block_of(g)
+        keys = jnp.concatenate([kh_ref[:, at], kl_ref[:, at]], axis=0)
+        queries = stack_heads(q_ref, g)
+        out_grad, prob_grad = later
+        if g + 1 < KVH:
+            later = grads_of(g + 1)
         soft = p_ref[g]
-        prob_grad = dot(values, out_grad, NT)
         wide = soft.astype(jnp.float32)
         delta = jnp.sum(wide * prob_grad, axis=0, keepdims=True)
         score_grad = (wide * ((prob_grad - delta) * HD ** (-0.5))).astype(jnp.bfloat16)

time: 121 us -> 120 us (level)
  no operation moved by 1% of the time
where the time goes in v4:
time: 120 us; the launch traced here: 119 us
  blocking collectives  66.3 us (55%)
  starting transfers between devices  26.5 us (22%)
  Pallas kernels  12.2 us (10%)
  waiting for transfers between devices  8.12 us (7%)
  local copies, waits for them, and re-layouts  5.01 us (4%)
    all_to_all x3, blocking collectives, exchange(): return lax.all_to_all(block, axes, 0, 0, tiled=True)  66.3 us
    ppermute x4, starting transfers between devices, along_seq(): return lax.ppermute(block, ('h', 'c'), route)  22.1 us
    all_to_all x1, waiting for transfers between devices, exchange(): return lax.all_to_all(block, axes, 0, 0, tiled=True)  8.11 us
    pallas_call x1, Pallas kernels, per_device(): pl.pallas_call(backward_kernel, in_specs=[SM] * 2 + [VM] * 8, out_specs=[...  6.35 us
    unnamed x16, local copies, waits for them, and re-layouts  5.01 us
    all_to_all x1, starting transfers between devices, exchange(): return lax.all_to_all(block, axes, 0, 0, tiled=True)  4.43 us
    pallas_call x1, Pallas kernels, per_device(): pl.pallas_call(forward_kernel, in_specs=[SM] * 2 + [VM] * 8, out_specs=[V...  3.38 us
  transfers between devices with their start and end apart: 5, of which 1 were waited for; matrix products, arithmetic and copies ran while one was open for 0% of the time, Pallas kernels for 1%

profile of v4, /device:TPU:1, one launch (start us, length us, event | category | flops | bytes accessed | tf_op | source)
XLA Modules:
  0.0 118.9 jit_solution(14399099616756069262)
XLA Ops:
  0.6 16.2 %collective-permute-start = (bf16[128,1024]{1,0:T(8,128)(2,1)}, bf16[128,1024]{1,0:T(8,128)(2,1)S(1)}, u32[]{:S(2)}, u32[]{:S(2)}) collective-permute-start(bf16[128,1024]{1,0:T(8,128)(2,1)} %kl_hbm.1), channel_id=1, source_target_pairs={{0,1},{1,2},{2,3},{4,5},{5,6},{6,7},{8,9},{9,10},{10,11},{12,13},{... | collective-permute-start | bytes 786440 | tf_op jit(solution)/shard_map/ppermute | solution.py:342
  16.9 1.9 %collective-permute-start.1 = (bf16[128,1024]{1,0:T(8,128)(2,1)}, bf16[128,1024]{1,0:T(8,128)(2,1)S(1)}, u32[]{:S(2)}, u32[]{:S(2)}) collective-permute-start(bf16[128,1024]{1,0:T(8,128)(2,1)} %vl_hbm.1), channel_id=1, source_target_pairs={{0,1},{1,2},{2,3},{4,5},{5,6},{6,7},{8,9},{9,10},{10,11},{12,13},{... | collective-permute-start | bytes 786440 | tf_op jit(solution)/shard_map/ppermute | solution.py:342
  18.8 0.0 copy-start
  18.8 1.2 %copy-done = bf16[128,4096]{1,0:T(8,128)(2,1)S(1)} copy-done((bf16[128,4096]{1,0:T(8,128)(2,1)S(1)}, bf16[128,4096]{1,0:T(8,128)(2,1)}, u32[]{:S(2)}) %copy-start) | copy-done | bytes 1048600
  20.0 0.0 copy-start.1
  20.0 1.2 %copy-done.1 = bf16[128,4096]{1,0:T(8,128)(2,1)S(1)} copy-done((bf16[128,4096]{1,0:T(8,128)(2,1)S(1)}, bf16[128,4096]{1,0:T(8,128)(2,1)}, u32[]{:S(2)}) %copy-start.1) | copy-done | bytes 1048600
  21.3 0.0 copy-start.2
  21.3 0.9 copy-done.2
  22.2 0.0 copy-start.3
  22.2 0.9 copy-done.3
  23.2 0.0 copy-start.7
  23.2 0.7 copy-done.7
  23.8 0.0 copy-start.4
  23.8 0.0 copy-start.5
  23.8 0.0 copy-start.6
  23.8 1.3 %local.1 = (bf16[128,4096]{1,0:T(8,128)(2,1)S(1)}, bf16[128,1024]{1,0:T(8,128)(2,1)S(1)}, bf16[128,1024]{1,0:T(8,128)(2,1)S(1)}, bf16[128,4096]{1,0:T(8,128)(2,1)S(1)}, f32[8,128,512]{2,1,0:T(8,128)S(1)}) custom-call(s32[1,8]{1,0:T(1,128)S(1)} %copy-done.7, bf16[128,4096]{1,0:T(8,128)(2,1)S(1)} %copy-done, bf16[128,1024]{1,0:T(8,128)(2,1)S(1)} %copy-done.2, ...), custom_call_target="tpu_custom_call" | custom-call | flops 140000000 | bytes 8000000 | tf_op jit(solution)/shard_map/local/pallas_call | solution.py:357
  25.1 0.0 collective-permute-done.kh_ref
  25.1 0.0 collective-permute-done.1.vh_ref
  25.1 0.0 copy-done.4
  25.2 0.0 copy-done.5
  25.2 0.0 copy-done.6
  25.2 3.4 %forward.1 = (bf16[8,256,512]{2,1,0:T(8,128)(2,1)S(1)}, f32[128,4096]{1,0:T(8,128)S(1)}, f32[12,8,512]{2,1,0:T(8,128)S(1)}) custom-call(s32[1,8]{1,0:T(1,128)S(1)} %copy-done.7, s32[1536]{0:T(1024)S(1)} %copy-done.6, bf16[128,4096]{1,0:T(8,128)(2,1)S(1)} %get-tuple-element.26.q_ref, bf16[128,1024]{1,0:T(8,128)(2,1)S(1)} %collective-permute-done.kh_ref, ...), custom_call_target="tpu_custom_call" | custom-call | flops 400000000 | bytes 8000000 | tf_op jit(solution)/shard_map/forward/pallas_call | solution.py:370
  28.5 24.9 %all_to_all.26.r_ref = f32[12,8,512]{2,1,0:T(8,128)S(1)} all-to-all(f32[12,8,512]{2,1,0:T(8,128)S(1)} %get-tuple-element.30), channel_id=1, replica_groups=mesh['y'=8,'l'=6,'x'=4,'h'=2,'c'=2] {'l','h'}, dimensions={0} | all-to-all | bytes 393216 | tf_op jit(solution)/shard_map/all_to_all | solution.py:346
  53.4 0.2 turn.1
  53.6 27.2 %all_to_all.27.r_ref = f32[64,4,128]{2,1,0:T(4,128)S(1)} all-to-all(f32[64,4,128]{2,1,0:T(4,128)S(1)} %turn.1), channel_id=1, replica_groups=mesh['y'=8,'l'=6,'x'=4,'h'=2,'c'=2] {'y','x','c'}, dimensions={0} | all-to-all | bytes 262144 | tf_op jit(solution)/shard_map/all_to_all | solution.py:346
  80.9 6.3 %backward.1 = (bf16[128,4096]{1,0:T(8,128)(2,1)}, bf16[128,2048]{1,0:T(8,128)(2,1)S(1)}, bf16[128,1024]{1,0:T(8,128)(2,1)S(1)}, bf16[128,1024]{1,0:T(8,128)(2,1)...) custom-call(s32[1,8]{1,0:T(1,128)S(1)} %copy-done.7, s32[1536]{0:T(1024)S(1)} %copy-done.6, f32[64,4,128]{2,1,0:T(4,128)S(1)} %all_to_all.27.r_ref, ...), custom_call_target="tpu_custom_call" | custom-call | flops 1080000000 | bytes 9000000 | tf_op jit(solution)/shard_map/backward/pallas_call | solution.py:398
  87.2 4.4 %all-to-all-start.2 = ((f32[64,1,128]{2,1,0:T(1,128)}), f32[64,1,128]{2,1,0:T(1,128)S(1)}, u32[]{:S(2)}, u32[]{:S(2)}) async-start(f32[64,1,128]{2,1,0:T(1,128)} %bitcast.4), calls=%async_computation.2 | async-start | bytes 65536 | tf_op jit(solution)/shard_map/all_to_all | solution.py:346
  91.6 1.3 %collective-permute-start.2 = (bf16[128,2048]{1,0:T(8,128)(2,1)S(1)}, bf16[128,2048]{1,0:T(8,128)(2,1)S(1)}, u32[]{:S(2)}, u32[]{:S(2)}) collective-permute-start(bf16[128,2048]{1,0:T(8,128)(2,1)S(1)} %get-tuple-element.41), channel_id=1, source_target_pairs={{2,1},{6,5},{10,9},{14,13},{18,17},{22,21},{26,25},{30,29},{34,33}... | collective-permute-start | bytes 1572872 | tf_op jit(solution)/shard_map/ppermute | solution.py:342
  92.9 8.1 %all-to-all-done.2 = f32[64,1,128]{2,1,0:T(1,128)S(1)} async-done(((f32[64,1,128]{2,1,0:T(1,128)}), f32[64,1,128]{2,1,0:T(1,128)S(1)}, u32[]{:S(2)}, u32[]{:S(2)}) %all-to-all-start.2) | async-done | bytes 32800 | tf_op jit(solution)/shard_map/all_to_all | solution.py:346
  101.1 0.1 pass.1
  101.1 2.6 %collective-permute-start.3 = (bf16[128,2048]{1,0:T(8,128)(2,1)S(1)}, bf16[128,2048]{1,0:T(8,128)(2,1)S(1)}, u32[]{:S(2)}, u32[]{:S(2)}) collective-permute-start(bf16[128,2048]{1,0:T(8,128)(2,1)S(1)} %get-tuple-element.41), channel_id=1, source_target_pairs={{1,0},{3,2},{5,4},{7,6},{9,8},{11,10},{13,12},{15,14},{17,16},{19,... | collective-permute-start | bytes 1572872 | tf_op jit(solution)/shard_map/ppermute | solution.py:342
  103.8 14.2 %all_to_all.28.r_ref = f32[12,4,128]{2,1,0:T(4,128)S(1)} all-to-all(f32[12,4,128]{2,1,0:T(4,128)S(1)} %pass.1), channel_id=1, replica_groups=mesh['y'=8,'l'=6,'x'=4,'h'=2,'c'=2] {'l','h'}, dimensions={0} | all-to-all | bytes 49152 | tf_op jit(solution)/shard_map/all_to_all | solution.py:346
  117.9 0.0 collective-permute-done.2.across_ref
  117.9 0.0 collective-permute-done.3.beside_ref
  117.9 1.0 finish.1
Async XLA Ops:
  0.6 24.5 %collective-permute-start = (bf16[128,1024]{1,0:T(8,128)(2,1)}, bf16[128,1024]{1,0:T(8,128)(2,1)S(1)}, u32[]{:S(2)}, u32[]{:S(2)}) collective-permute-start(bf16[128,1024]{1,0:T(8,128)(2,1)} %kl_hbm.1), channel_id=1, source_target_pairs={{0,1},{1,2},{2,3},{4,5},{5,6},{6,7},{8,9},{9,10},{10,11},{12,13},{... | collective-permute-start | bytes 786440 | tf_op jit(solution)/shard_map/ppermute | solution.py:342
  16.9 8.2 %collective-permute-start.1 = (bf16[128,1024]{1,0:T(8,128)(2,1)}, bf16[128,1024]{1,0:T(8,128)(2,1)S(1)}, u32[]{:S(2)}, u32[]{:S(2)}) collective-permute-start(bf16[128,1024]{1,0:T(8,128)(2,1)} %vl_hbm.1), channel_id=1, source_target_pairs={{0,1},{1,2},{2,3},{4,5},{5,6},{6,7},{8,9},{9,10},{10,11},{12,13},{... | collective-permute-start | bytes 786440 | tf_op jit(solution)/shard_map/ppermute | solution.py:342
  18.8 1.2 %copy-start = (bf16[128,4096]{1,0:T(8,128)(2,1)S(1)}, bf16[128,4096]{1,0:T(8,128)(2,1)}, u32[]{:S(2)}) copy-start(bf16[128,4096]{1,0:T(8,128)(2,1)} %q_hbm.1) | copy-start | bytes 3145732
  20.0 1.2 %copy-start.1 = (bf16[128,4096]{1,0:T(8,128)(2,1)S(1)}, bf16[128,4096]{1,0:T(8,128)(2,1)}, u32[]{:S(2)}) copy-start(bf16[128,4096]{1,0:T(8,128)(2,1)} %res_hbm.1) | copy-start | bytes 3145732
  21.3 0.9 copy-start.2
  22.2 0.9 copy-start.3
  23.2 0.7 copy-start.7
  23.8 1.3 %copy-start.4 = (f32[4096]{0:T(1024)S(1)}, f32[4096]{0:T(1024)}, u32[]{:S(2)}) copy-start(f32[4096]{0:T(1024)} %param.12) | copy-start | bytes 49156
  23.8 1.3 %copy-start.5 = (f32[4096]{0:T(1024)S(1)}, f32[4096]{0:T(1024)}, u32[]{:S(2)}) copy-start(f32[4096]{0:T(1024)} %param.13) | copy-start | bytes 49156
  23.8 1.3 %copy-start.6 = (s32[1536]{0:T(1024)S(1)}, s32[1536]{0:T(1024)}, u32[]{:S(2)}) copy-start(s32[1536]{0:T(1024)} %slot_ref.3) | copy-start | bytes 18436
  87.2 13.8 %all-to-all-start.2 = ((f32[64,1,128]{2,1,0:T(1,128)}), f32[64,1,128]{2,1,0:T(1,128)S(1)}, u32[]{:S(2)}, u32[]{:S(2)}) async-start(f32[64,1,128]{2,1,0:T(1,128)} %bitcast.4), calls=%async_computation.2 | async-start | bytes 65536 | tf_op jit(solution)/shard_map/all_to_all | solution.py:346
  91.6 26.3 %collective-permute-start.2 = (bf16[128,2048]{1,0:T(8,128)(2,1)S(1)}, bf16[128,2048]{1,0:T(8,128)(2,1)S(1)}, u32[]{:S(2)}, u32[]{:S(2)}) collective-permute-start(bf16[128,2048]{1,0:T(8,128)(2,1)S(1)} %get-tuple-element.41), channel_id=1, source_target_pairs={{2,1},{6,5},{10,9},{14,13},{18,17},{22,21},{26,25},{30,29},{34,33}... | collective-permute-start | bytes 1572872 | tf_op jit(solution)/shard_map/ppermute | solution.py:342
  101.1 16.8 %collective-permute-start.3 = (bf16[128,2048]{1,0:T(8,128)(2,1)S(1)}, bf16[128,2048]{1,0:T(8,128)(2,1)S(1)}, u32[]{:S(2)}, u32[]{:S(2)}) collective-permute-start(bf16[128,2048]{1,0:T(8,128)(2,1)S(1)} %get-tuple-element.41), channel_id=1, source_target_pairs={{1,0},{3,2},{5,4},{7,6},{9,8},{11,10},{13,12},{15,14},{17,16},{19,... | collective-permute-start | bytes 1572872 | tf_op jit(solution)/shard_map/ppermute | solution.py:342

commit v5 on v4

--- a/solution.py
+++ b/solution.py
@@ -22,6 +22,7 @@
 N_PLANE = NY * NX * NC
 N_RING = NL * NH
 COLUMNS = NY * NX
+PAIRS = COLUMNS // 2
 WIDE = 384
 PER = 3
 
@@ -210,13 +211,14 @@
     got = r_ref[...].reshape(COLUMNS, NC, PER + 1, LANES)
     sum_ref[...] = got[:, 0] + got[:, 1]
     extra = sum_ref[:, PER, :]
-    lane32 = lax.broadcasted_iota(jnp.int32, (COLUMNS, LANES), 1)
-    slots = jnp.where(lane32 < 64, pltpu.roll(extra, 64, 1), extra).astype(jnp.int32)
-    rewards = jnp.where(lane32 < 64, extra, 0.0)
+    top, bottom = extra[:PAIRS], extra[PAIRS:]
+    lower_half = lax.broadcasted_iota(jnp.int32, (PAIRS, LANES), 1) < 64
+    slots = jnp.where(lower_half, pltpu.roll(top, 64, 1), bottom).astype(jnp.int32)
+    rewards = jnp.where(lower_half, top, pltpu.roll(bottom, 64, 1))
     lower = lax.broadcasted_iota(jnp.int32, (PROMPTS, LANES), 0)
     rank = lax.broadcasted_iota(jnp.int32, (GROUP, LANES), 0)
     spread, onehot, ranked = [], [], []
-    for at in range(COLUMNS):
+    for at in range(PAIRS):
         slot = slots[at : at + 1]
         onehot.append(jnp.where(lower == (slot >> 4), 1.0, 0.0).astype(jnp.bfloat16))
         same = rank == (slot & 15)
@@ -239,19 +241,6 @@
         runs.append(runs[-1] + inverse[r : r + 1])
     grid_grad = raised * jnp.concatenate(runs, axis=0) - 1.0
     pieces = jnp.concatenate(split3(grid_grad), axis=0)
-    found = dot(pieces, onehot, NN)
-    total = jnp.zeros((PER + 1, LANES), jnp.float32)
-    for at in range(COLUMNS):
-        part = found[:, at * LANES : (at + 1) * LANES]
-        part = (part[0:16] + (part[16:32] + part[32:48])) * ranked[at]
-        total = total + sum_ref[at] * jnp.sum(part, axis=0, keepdims=True)
-    row = lax.broadcasted_iota(jnp.int32, (PER + 1, LANES), 0)
-    lane = lax.broadcasted_iota(jnp.int32, (PER + 1, LANES), 1)
-    first = jnp.sum(jnp.where(lane < 64, total, 0.0), axis=1, keepdims=True)
-    second = jnp.sum(jnp.where(lane < 64, 0.0, total), axis=1, keepdims=True)
-    placed = jnp.where(row == lane, first, 0.0) + jnp.where(row + PER == lane, second, 0.0)
-    placed = jnp.sum(jnp.where(row < PER, placed, 0.0), axis=0, keepdims=True)
-    x_ref[...] = jnp.broadcast_to(placed, (N_PLANE, LANES))
     rows = lax.broadcasted_iota(jnp.int32, (TOK, PROMPTS), 0)
     doc = doc_of(rows + seq * TOK, ends)
     slots = pick(doc, [slot_ref[window * DOCS + j] for j in range(DOCS)], jnp.int32)
@@ -262,6 +251,27 @@
     found = jnp.where((lanes & 15) == (slots[:, :48] & 15), found, 0.0)
     lengths = [len_ref[0, j].astype(jnp.float32) for j in range(DOCS)]
     token_grad = jnp.sum(found, axis=1, keepdims=True) / pick(doc[:, :1], lengths, jnp.float32)
+    found = dot(pieces, onehot, NN)
+    doc_grad = []
+    for at in range(PAIRS):
+        part = found[:, at * LANES : (at + 1) * LANES]
+        part = (part[0:16] + (part[16:32] + part[32:48])) * ranked[at]
+        doc_grad.append(jnp.sum(part, axis=0, keepdims=True))
+    doc_grad = jnp.concatenate(doc_grad, axis=0)
+    turned = pltpu.roll(doc_grad, 64, 1)
+    first = jnp.where(lower_half, doc_grad, turned)
+    second = jnp.where(lower_half, turned, doc_grad)
+    total = jnp.zeros((PER + 1, LANES), jnp.float32)
+    for at in range(PAIRS):
+        total = total + sum_ref[at] * first[at : at + 1]
+        total = total + sum_ref[PAIRS + at] * second[at : at + 1]
+    row = lax.broadcasted_iota(jnp.int32, (PER + 1, LANES), 0)
+    lane = lax.broadcasted_iota(jnp.int32, (PER + 1, LANES), 1)
+    first = jnp.sum(jnp.where(lane < 64, total, 0.0), axis=1, keepdims=True)
+    second = jnp.sum(jnp.where(lane < 64, 0.0, total), axis=1, keepdims=True)
+    placed = jnp.where(row == lane, first, 0.0) + jnp.where(row + PER == lane, second, 0.0)
+    placed = jnp.sum(jnp.where(row < PER, placed, 0.0), axis=0, keepdims=True)
+    x_ref[...] = jnp.broadcast_to(placed, (N_PLANE, LANES))
     leaving = []
     def grads_of(g):
         out_grad = jnp.concatenate(

time: 120 us -> 119 us (level)
  no operation moved by 1% of the time
where the time goes in v5:
time: 119 us; the launch traced here: 118 us
  blocking collectives  66.3 us (56%)
  starting transfers between devices  26.5 us (22%)
  Pallas kernels  11.7 us (10%)
  waiting for transfers between devices  8.12 us (7%)
  local copies, waits for them, and re-layouts  5.01 us (4%)
    all_to_all x3, blocking collectives, exchange(): return lax.all_to_all(block, axes, 0, 0, tiled=True)  66.3 us
    ppermute x4, starting transfers between devices, along_seq(): return lax.ppermute(block, ('h', 'c'), route)  22.1 us
    all_to_all x1, waiting for transfers between devices, exchange(): return lax.all_to_all(block, axes, 0, 0, tiled=True)  8.11 us
    pallas_call x1, Pallas kernels, per_device(): pl.pallas_call(backward_kernel, in_specs=[SM] * 2 + [VM] * 8, out_specs=[...  5.8 us
    unnamed x16, local copies, waits for them, and re-layouts  5.01 us
    all_to_all x1, starting transfers between devices, exchange(): return lax.all_to_all(block, axes, 0, 0, tiled=True)  4.43 us
    pallas_call x1, Pallas kernels, per_device(): pl.pallas_call(forward_kernel, in_specs=[SM] * 2 + [VM] * 8, out_specs=[V...  3.38 us
  transfers between devices with their start and end apart: 5, of which 1 were waited for; matrix products, arithmetic and copies ran while one was open for 0% of the time, Pallas kernels for 1%

profile of v5, /device:TPU:1, one launch (start us, length us, event | category | flops | bytes accessed | tf_op | source)
XLA Modules:
  0.0 118.4 jit_solution(3705287065429809308)
XLA Ops:
  0.6 16.2 %collective-permute-start = (bf16[128,1024]{1,0:T(8,128)(2,1)}, bf16[128,1024]{1,0:T(8,128)(2,1)S(1)}, u32[]{:S(2)}, u32[]{:S(2)}) collective-permute-start(bf16[128,1024]{1,0:T(8,128)(2,1)} %kl_hbm.1), channel_id=1, source_target_pairs={{0,1},{1,2},{2,3},{4,5},{5,6},{6,7},{8,9},{9,10},{10,11},{12,13},{... | collective-permute-start | bytes 786440 | tf_op jit(solution)/shard_map/ppermute | solution.py:352
  16.9 1.9 %collective-permute-start.1 = (bf16[128,1024]{1,0:T(8,128)(2,1)}, bf16[128,1024]{1,0:T(8,128)(2,1)S(1)}, u32[]{:S(2)}, u32[]{:S(2)}) collective-permute-start(bf16[128,1024]{1,0:T(8,128)(2,1)} %vl_hbm.1), channel_id=1, source_target_pairs={{0,1},{1,2},{2,3},{4,5},{5,6},{6,7},{8,9},{9,10},{10,11},{12,13},{... | collective-permute-start | bytes 786440 | tf_op jit(solution)/shard_map/ppermute | solution.py:352
  18.8 0.0 copy-start
  18.8 1.2 %copy-done = bf16[128,4096]{1,0:T(8,128)(2,1)S(1)} copy-done((bf16[128,4096]{1,0:T(8,128)(2,1)S(1)}, bf16[128,4096]{1,0:T(8,128)(2,1)}, u32[]{:S(2)}) %copy-start) | copy-done | bytes 1048600
  20.0 0.0 copy-start.1
  20.0 1.2 %copy-done.1 = bf16[128,4096]{1,0:T(8,128)(2,1)S(1)} copy-done((bf16[128,4096]{1,0:T(8,128)(2,1)S(1)}, bf16[128,4096]{1,0:T(8,128)(2,1)}, u32[]{:S(2)}) %copy-start.1) | copy-done | bytes 1048600
  21.3 0.0 copy-start.2
  21.3 0.9 copy-done.2
  22.2 0.0 copy-start.3
  22.2 0.9 copy-done.3
  23.2 0.0 copy-start.7
  23.2 0.7 copy-done.7
  23.8 0.0 copy-start.4
  23.8 0.0 copy-start.5
  23.8 0.0 copy-start.6
  23.8 1.3 %local.1 = (bf16[128,4096]{1,0:T(8,128)(2,1)S(1)}, bf16[128,1024]{1,0:T(8,128)(2,1)S(1)}, bf16[128,1024]{1,0:T(8,128)(2,1)S(1)}, bf16[128,4096]{1,0:T(8,128)(2,1)S(1)}, f32[8,128,512]{2,1,0:T(8,128)S(1)}) custom-call(s32[1,8]{1,0:T(1,128)S(1)} %copy-done.7, bf16[128,4096]{1,0:T(8,128)(2,1)S(1)} %copy-done, bf16[128,1024]{1,0:T(8,128)(2,1)S(1)} %copy-done.2, ...), custom_call_target="tpu_custom_call" | custom-call | flops 140000000 | bytes 8000000 | tf_op jit(solution)/shard_map/local/pallas_call | solution.py:367
  25.1 0.0 collective-permute-done.kh_ref
  25.1 0.0 collective-permute-done.1.vh_ref
  25.1 0.0 copy-done.4
  25.2 0.0 copy-done.5
  25.2 0.0 copy-done.6
  25.2 3.4 %forward.1 = (bf16[8,256,512]{2,1,0:T(8,128)(2,1)S(1)}, f32[128,4096]{1,0:T(8,128)S(1)}, f32[12,8,512]{2,1,0:T(8,128)S(1)}) custom-call(s32[1,8]{1,0:T(1,128)S(1)} %copy-done.7, s32[1536]{0:T(1024)S(1)} %copy-done.6, bf16[128,4096]{1,0:T(8,128)(2,1)S(1)} %get-tuple-element.26.q_ref, bf16[128,1024]{1,0:T(8,128)(2,1)S(1)} %collective-permute-done.kh_ref, ...), custom_call_target="tpu_custom_call" | custom-call | flops 400000000 | bytes 8000000 | tf_op jit(solution)/shard_map/forward/pallas_call | solution.py:380
  28.5 24.9 %all_to_all.26.r_ref = f32[12,8,512]{2,1,0:T(8,128)S(1)} all-to-all(f32[12,8,512]{2,1,0:T(8,128)S(1)} %get-tuple-element.30), channel_id=1, replica_groups=mesh['y'=8,'l'=6,'x'=4,'h'=2,'c'=2] {'l','h'}, dimensions={0} | all-to-all | bytes 393216 | tf_op jit(solution)/shard_map/all_to_all | solution.py:356
  53.4 0.2 turn.1
  53.6 27.2 %all_to_all.27.r_ref = f32[64,4,128]{2,1,0:T(4,128)S(1)} all-to-all(f32[64,4,128]{2,1,0:T(4,128)S(1)} %turn.1), channel_id=1, replica_groups=mesh['y'=8,'l'=6,'x'=4,'h'=2,'c'=2] {'y','x','c'}, dimensions={0} | all-to-all | bytes 262144 | tf_op jit(solution)/shard_map/all_to_all | solution.py:356
  80.9 5.8 %backward.1 = (bf16[128,4096]{1,0:T(8,128)(2,1)}, bf16[128,2048]{1,0:T(8,128)(2,1)S(1)}, bf16[128,1024]{1,0:T(8,128)(2,1)S(1)}, bf16[128,1024]{1,0:T(8,128)(2,1)...) custom-call(s32[1,8]{1,0:T(1,128)S(1)} %copy-done.7, s32[1536]{0:T(1024)S(1)} %copy-done.6, f32[64,4,128]{2,1,0:T(4,128)S(1)} %all_to_all.27.r_ref, ...), custom_call_target="tpu_custom_call" | custom-call | flops 1080000000 | bytes 9000000 | tf_op jit(solution)/shard_map/backward/pallas_call | solution.py:408
  86.7 4.4 %all-to-all-start.2 = ((f32[64,1,128]{2,1,0:T(1,128)}), f32[64,1,128]{2,1,0:T(1,128)S(1)}, u32[]{:S(2)}, u32[]{:S(2)}) async-start(f32[64,1,128]{2,1,0:T(1,128)} %bitcast.4), calls=%async_computation.2 | async-start | bytes 65536 | tf_op jit(solution)/shard_map/all_to_all | solution.py:356
  91.1 1.3 %collective-permute-start.2 = (bf16[128,2048]{1,0:T(8,128)(2,1)S(1)}, bf16[128,2048]{1,0:T(8,128)(2,1)S(1)}, u32[]{:S(2)}, u32[]{:S(2)}) collective-permute-start(bf16[128,2048]{1,0:T(8,128)(2,1)S(1)} %get-tuple-element.41), channel_id=1, source_target_pairs={{2,1},{6,5},{10,9},{14,13},{18,17},{22,21},{26,25},{30,29},{34,33}... | collective-permute-start | bytes 1572872 | tf_op jit(solution)/shard_map/ppermute | solution.py:352
  92.4 8.1 %all-to-all-done.2 = f32[64,1,128]{2,1,0:T(1,128)S(1)} async-done(((f32[64,1,128]{2,1,0:T(1,128)}), f32[64,1,128]{2,1,0:T(1,128)S(1)}, u32[]{:S(2)}, u32[]{:S(2)}) %all-to-all-start.2) | async-done | bytes 32800 | tf_op jit(solution)/shard_map/all_to_all | solution.py:356
  100.5 0.1 pass.1
  100.6 2.6 %collective-permute-start.3 = (bf16[128,2048]{1,0:T(8,128)(2,1)S(1)}, bf16[128,2048]{1,0:T(8,128)(2,1)S(1)}, u32[]{:S(2)}, u32[]{:S(2)}) collective-permute-start(bf16[128,2048]{1,0:T(8,128)(2,1)S(1)} %get-tuple-element.41), channel_id=1, source_target_pairs={{1,0},{3,2},{5,4},{7,6},{9,8},{11,10},{13,12},{15,14},{17,16},{19,... | collective-permute-start | bytes 1572872 | tf_op jit(solution)/shard_map/ppermute | solution.py:352
  103.2 14.2 %all_to_all.28.r_ref = f32[12,4,128]{2,1,0:T(4,128)S(1)} all-to-all(f32[12,4,128]{2,1,0:T(4,128)S(1)} %pass.1), channel_id=1, replica_groups=mesh['y'=8,'l'=6,'x'=4,'h'=2,'c'=2] {'l','h'}, dimensions={0} | all-to-all | bytes 49152 | tf_op jit(solution)/shard_map/all_to_all | solution.py:356
  117.4 0.0 collective-permute-done.2.across_ref
  117.4 0.0 collective-permute-done.3.beside_ref
  117.4 1.0 finish.1
Async XLA Ops:
  0.6 24.5 %collective-permute-start = (bf16[128,1024]{1,0:T(8,128)(2,1)}, bf16[128,1024]{1,0:T(8,128)(2,1)S(1)}, u32[]{:S(2)}, u32[]{:S(2)}) collective-permute-start(bf16[128,1024]{1,0:T(8,128)(2,1)} %kl_hbm.1), channel_id=1, source_target_pairs={{0,1},{1,2},{2,3},{4,5},{5,6},{6,7},{8,9},{9,10},{10,11},{12,13},{... | collective-permute-start | bytes 786440 | tf_op jit(solution)/shard_map/ppermute | solution.py:352
  16.9 8.2 %collective-permute-start.1 = (bf16[128,1024]{1,0:T(8,128)(2,1)}, bf16[128,1024]{1,0:T(8,128)(2,1)S(1)}, u32[]{:S(2)}, u32[]{:S(2)}) collective-permute-start(bf16[128,1024]{1,0:T(8,128)(2,1)} %vl_hbm.1), channel_id=1, source_target_pairs={{0,1},{1,2},{2,3},{4,5},{5,6},{6,7},{8,9},{9,10},{10,11},{12,13},{... | collective-permute-start | bytes 786440 | tf_op jit(solution)/shard_map/ppermute | solution.py:352
  18.8 1.2 %copy-start = (bf16[128,4096]{1,0:T(8,128)(2,1)S(1)}, bf16[128,4096]{1,0:T(8,128)(2,1)}, u32[]{:S(2)}) copy-start(bf16[128,4096]{1,0:T(8,128)(2,1)} %q_hbm.1) | copy-start | bytes 3145732
  20.0 1.2 %copy-start.1 = (bf16[128,4096]{1,0:T(8,128)(2,1)S(1)}, bf16[128,4096]{1,0:T(8,128)(2,1)}, u32[]{:S(2)}) copy-start(bf16[128,4096]{1,0:T(8,128)(2,1)} %res_hbm.1) | copy-start | bytes 3145732
  21.3 0.9 copy-start.2
  22.2 0.9 copy-start.3
  23.2 0.7 copy-start.7
  23.8 1.3 %copy-start.4 = (f32[4096]{0:T(1024)S(1)}, f32[4096]{0:T(1024)}, u32[]{:S(2)}) copy-start(f32[4096]{0:T(1024)} %param.12) | copy-start | bytes 49156
  23.8 1.3 %copy-start.5 = (f32[4096]{0:T(1024)S(1)}, f32[4096]{0:T(1024)}, u32[]{:S(2)}) copy-start(f32[4096]{0:T(1024)} %param.13) | copy-start | bytes 49156
  23.8 1.3 %copy-start.6 = (s32[1536]{0:T(1024)S(1)}, s32[1536]{0:T(1024)}, u32[]{:S(2)}) copy-start(s32[1536]{0:T(1024)} %slot_ref.3) | copy-start | bytes 18436
  86.7 13.8 %all-to-all-start.2 = ((f32[64,1,128]{2,1,0:T(1,128)}), f32[64,1,128]{2,1,0:T(1,128)S(1)}, u32[]{:S(2)}, u32[]{:S(2)}) async-start(f32[64,1,128]{2,1,0:T(1,128)} %bitcast.4), calls=%async_computation.2 | async-start | bytes 65536 | tf_op jit(solution)/shard_map/all_to_all | solution.py:356
  91.1 26.3 %collective-permute-start.2 = (bf16[128,2048]{1,0:T(8,128)(2,1)S(1)}, bf16[128,2048]{1,0:T(8,128)(2,1)S(1)}, u32[]{:S(2)}, u32[]{:S(2)}) collective-permute-start(bf16[128,2048]{1,0:T(8,128)(2,1)S(1)} %get-tuple-element.41), channel_id=1, source_target_pairs={{2,1},{6,5},{10,9},{14,13},{18,17},{22,21},{26,25},{30,29},{34,33}... | collective-permute-start | bytes 1572872 | tf_op jit(solution)/shard_map/ppermute | solution.py:352
  100.6 16.8 %collective-permute-start.3 = (bf16[128,2048]{1,0:T(8,128)(2,1)S(1)}, bf16[128,2048]{1,0:T(8,128)(2,1)S(1)}, u32[]{:S(2)}, u32[]{:S(2)}) collective-permute-start(bf16[128,2048]{1,0:T(8,128)(2,1)S(1)} %get-tuple-element.41), channel_id=1, source_target_pairs={{1,0},{3,2},{5,4},{7,6},{9,8},{11,10},{13,12},{15,14},{17,16},{19,... | collective-permute-start | bytes 1572872 | tf_op jit(solution)/shard_map/ppermute | solution.py:352
